TPU v7x, 32 devices: a whole 2x2x4 slice. The times are simulated.
32 devices in a mesh: ens: 4 (over x, core), grid: 8 (over z, y).
Axes of the slice: x: 2, y: 2, z: 4, core: 2. Of those that a mesh axis runs over, the one named last changes fastest.
Arguments:
- embeddings: bfloat16 [8, 1024, 1024], P('ens', 'grid'), may hold values from -20 to 20
- reference_analysis: float32 [100, 1024], P(None, 'grid'), may hold values from -6 to 6
- attention_matrix: bfloat16 [1024, 3072], replicated, may hold values from -8 to 8
- readout_matrix: bfloat16 [1024, 100], replicated, may hold values from -0.1875 to 0.1875
- adjacent_blocks: int32 [16, 3], P('grid'), may hold values from 0 to 15, as said below
- companion_matrix: int32 [7, 8], replicated, may hold values from 0 to 7, as said below
- continent_indicator: int32 [1024], P('grid'), may hold values 0 or 1
- zonal_strip: int32 [1024], P('grid'), may hold values from 0 to 720
Outputs:
- energy_objective: float32 [], replicated
- embedding_sensitivity: float32 [8, 1024, 1024], P('ens', 'grid')
- grad_value_matrix: float32 [1048576], P(('ens', 'grid'))
- grad_dec: float32 [102400], P(('ens', 'grid'))
Inputs may be any that keep to these rules, and one draw needn't show every extreme that they name: `adjacent_blocks`: entry 0 of row b is b; entry 1 lies 1 to 2 blocks before b and entry 2 lies 1 to 2 blocks after b, each clamped into 0 to 15. Each row is a perfect matching of the members: companion_matrix[r, companion_matrix[r, m]] = m and companion_matrix[r, m] != m; every two members are partners in exactly one row.
All inputs are finite; a program needn't handle non-finite values. No bound on the sum of `continent_indicator` on one device may be relied on, other than what follows from the above.
Results may differ from a plain program's by a relative error of at most 0.012.
The roundings to bfloat16 on the way count: a program that leaves them out, or rounds other values in their place, can miss the bound.
Values may be sent and summed in bfloat16 or wider, within the bound.
A program may use at most 128 MiB of HBM per device.

v0:
```python
import math

import jax
import jax.numpy as jnp
from jax import lax
from jax.sharding import PartitionSpec as P

HEADS = 16
QB = 64
R_BLK = 2
NB = 3
SCORED_ENTRIES = 128
NLAT = 721


EPSILON = 1e-06


def with_halo(value, sides, width):
    for axis, dim in sides:
        size, length = (lax.axis_size(axis), value.shape[dim])
        up = [(i, (i + 1) % size) for i in range(size - 1)]
        down = [(j, i) for i, j in up]
        last = lax.slice_in_dim(value, length - width, length, axis=dim)
        leading = lax.slice_in_dim(value, 0, width, axis=dim)
        before = lax.ppermute(last, axis, up)
        after = lax.ppermute(leading, axis, down)
        value = jnp.concatenate([before, value, after], axis=dim)
    return value


def passed_along(value, axis, steps):
    count = lax.axis_size(axis)
    leading, last = (max(0, -steps), min(count, count - steps))
    return lax.ppermute(value, axis, [(source, source + steps) for source in range(leading, last)])


def rms_scale(values):
    return lax.rsqrt(jnp.mean(values * values, axis=-1, keepdims=True) + EPSILON)


def per_device(
    embeddings,
    reference_analysis,
    attention_matrix,
    readout_matrix,
    adjacent_blocks,
    companion_matrix,
    continent_indicator,
    zonal_strip,
):
    members_per_part, patches_per_part, model_width = embeddings.shape
    variable_indices = reference_analysis.shape[0]
    blk_dev = patches_per_part // QB
    reach_blocks = R_BLK
    rim_rows = reach_blocks * QB
    ext_blocks = blk_dev + 2 * reach_blocks
    head_dim = model_width // HEADS
    score_scale = 1.0 / math.sqrt(head_dim)
    round_count = companion_matrix.shape[0]
    sample_count = companion_matrix.shape[1]
    shard_regions = patches_per_part // SCORED_ENTRIES
    lat_float = embeddings.astype(jnp.float32)
    inv_first = rms_scale(lat_float)
    normed = (lat_float * inv_first).astype(jnp.bfloat16)
    projected = jnp.einsum(
        "mpd,de->mpe", normed, attention_matrix, preferred_element_type=jnp.float32
    ).astype(jnp.bfloat16)
    queries = projected[:, :, :model_width]
    keyval = projected[:, :, model_width:]
    normed_ext = with_halo(normed, (("grid", 1),), rim_rows)
    rim_inputs = jnp.concatenate(
        [normed_ext[:, :rim_rows], normed_ext[:, rim_rows + patches_per_part :]], axis=1
    )
    rim_keyval = jnp.einsum(
        "mpd,de->mpe",
        rim_inputs,
        attention_matrix[:, model_width:],
        preferred_element_type=jnp.float32,
    ).astype(jnp.bfloat16)
    keyval_ext = jnp.concatenate(
        [rim_keyval[:, :rim_rows], keyval, rim_keyval[:, rim_rows:]], axis=1
    )
    first_block = lax.axis_index("grid") * blk_dev
    local_slots = (adjacent_blocks - first_block + reach_blocks).reshape(-1)
    ext_view = keyval_ext.reshape(members_per_part, ext_blocks, QB, 2 * model_width)
    picked = jnp.take(ext_view, local_slots, axis=1).reshape(
        members_per_part, blk_dev, NB * QB, 2, HEADS, head_dim
    )
    window_keys = picked[:, :, :, 0]
    window_values = picked[:, :, :, 1]
    query_blocks = queries.reshape(members_per_part, blk_dev, QB, HEADS, head_dim)
    scores = (
        jnp.einsum(
            "mbqhe,mbkhe->mbhqk", query_blocks, window_keys, preferred_element_type=jnp.float32
        )
        * score_scale
    )
    highest = jnp.max(scores, axis=-1, keepdims=True)
    exp_scores = jnp.exp(scores - highest)
    attention = exp_scores / jnp.sum(exp_scores, axis=-1, keepdims=True)
    attention16 = attention.astype(jnp.bfloat16)
    attended = jnp.einsum(
        "mbhqk,mbkhe->mbqhe", attention16, window_values, preferred_element_type=jnp.float32
    )
    residual_state = lat_float + attended.reshape(members_per_part, patches_per_part, model_width)
    inv_second = rms_scale(residual_state)
    internal_activation = (residual_state * inv_second).astype(jnp.bfloat16)
    predicted_grid = jnp.einsum(
        "qfo,or->qrf", internal_activation, readout_matrix, preferred_element_type=jnp.float32
    )
    phase = (zonal_strip.astype(jnp.float32) + 0.5) * (math.pi / NLAT) - 0.5 * math.pi
    location_factors = (jnp.cos(phase) * (1.0 + continent_indicator.astype(jnp.float32))).reshape(
        shard_regions, SCORED_ENTRIES
    )
    ensemble_outputs = lax.all_gather(predicted_grid, "ens", axis=0, tiled=True)
    own_ids = lax.axis_index("ens") * members_per_part + jnp.arange(
        members_per_part, dtype=jnp.int32
    )
    member_ids = jnp.arange(sample_count, dtype=jnp.int32)
    own_pick = (member_ids[None, :] == own_ids[:, None]).astype(jnp.int32)
    own_partners = jnp.sum(companion_matrix[None, :, :] * own_pick[:, None, :], axis=-1)
    patch_ids = lax.axis_index("grid") * shard_regions + jnp.arange(shard_regions, dtype=jnp.int32)
    round_of = (
        jnp.arange(variable_indices, dtype=jnp.int32)[:, None] + patch_ids[None, :]
    ) % round_count
    round_pick = (round_of[:, :, None] == jnp.arange(round_count, dtype=jnp.int32)).astype(
        jnp.int32
    )
    partner = jnp.sum(round_pick[None] * own_partners[:, None, None, :], axis=-1)
    partner_pick = (partner[..., None] == member_ids).astype(jnp.float32)
    region_indices = ensemble_outputs.reshape(
        sample_count, variable_indices, shard_regions, SCORED_ENTRIES
    )
    partner_patches = jnp.einsum(
        "mcjn,ncjp->mcjp", partner_pick, region_indices, precision=lax.Precision.HIGHEST
    )
    local_regions = predicted_grid.reshape(
        members_per_part, variable_indices, shard_regions, SCORED_ENTRIES
    )
    target_patches = reference_analysis.reshape(variable_indices, shard_regions, SCORED_ENTRIES)
    error_component = local_regions - target_patches[None]
    observed_separation = jnp.sqrt(
        jnp.sum(location_factors * error_component * error_component, axis=-1) + EPSILON
    )
    dispersion_component = local_regions - partner_patches
    mutual_separation = jnp.sqrt(
        jnp.sum(location_factors * dispersion_component * dispersion_component, axis=-1) + EPSILON
    )
    observed_sensitivity = location_factors * error_component / observed_separation[..., None]
    mutual_sensitivity = location_factors * dispersion_component / mutual_separation[..., None]
    bottom_portion = (own_ids[:, None, None] < partner).astype(jnp.float32)
    local_total = jnp.sum(observed_separation) - jnp.sum(bottom_portion * mutual_separation)
    outgoing = jnp.einsum(
        "mcjn,mcjp->ncjp",
        partner_pick,
        bottom_portion[..., None] * mutual_sensitivity,
        precision=lax.Precision.HIGHEST,
    )
    arriving_entries = lax.psum_scatter(outgoing, "ens", scatter_dimension=0, tiled=True)
    predicted_sensitivity = (
        observed_sensitivity - bottom_portion[..., None] * mutual_sensitivity + arriving_entries
    )
    total = lax.psum(local_total, ("ens", "grid"))
    energy_objective = total / (
        sample_count * variable_indices * shard_regions * lax.axis_size("grid")
    )
    sensitivity_reduced16 = predicted_sensitivity.reshape(
        members_per_part, variable_indices, patches_per_part
    ).astype(jnp.bfloat16)
    grad_dec_part = jnp.einsum(
        "mpd,mcp->dc",
        internal_activation,
        sensitivity_reduced16,
        preferred_element_type=jnp.float32,
    )
    grad_hidden = jnp.einsum(
        "mcp,dc->mpd", sensitivity_reduced16, readout_matrix, preferred_element_type=jnp.float32
    )
    unit_state = residual_state * inv_second
    grad_state = inv_second * (
        grad_hidden - unit_state * jnp.mean(grad_hidden * unit_state, axis=-1, keepdims=True)
    )
    grad_out16 = grad_state.astype(jnp.bfloat16).reshape(
        members_per_part, blk_dev, QB, HEADS, head_dim
    )
    grad_attention = jnp.einsum(
        "mbqhe,mbkhe->mbhqk", grad_out16, window_values, preferred_element_type=jnp.float32
    )
    grad_values = jnp.einsum(
        "mbhqk,mbqhe->mbkhe", attention16, grad_out16, preferred_element_type=jnp.float32
    )
    grad_scores = (
        attention
        * (grad_attention - jnp.sum(attention * grad_attention, axis=-1, keepdims=True))
        * score_scale
    ).astype(jnp.bfloat16)
    grad_queries = jnp.einsum(
        "mbhqk,mbkhe->mbqhe", grad_scores, window_keys, preferred_element_type=jnp.float32
    )
    grad_keys = jnp.einsum(
        "mbhqk,mbqhe->mbkhe", grad_scores, query_blocks, preferred_element_type=jnp.float32
    )
    grad_window = jnp.stack([grad_keys, grad_values], axis=3).reshape(
        members_per_part, blk_dev * NB, QB, 2 * model_width
    )
    slot_pick = (local_slots[:, None] == jnp.arange(ext_blocks, dtype=jnp.int32)[None, :]).astype(
        jnp.float32
    )
    grad_ext = jnp.einsum(
        "sn,msqc->mnqc", slot_pick, grad_window, precision=lax.Precision.HIGHEST
    ).reshape(members_per_part, ext_blocks * QB, 2 * model_width)
    before_rim = grad_ext[:, :rim_rows]
    after_rim = grad_ext[:, rim_rows + patches_per_part :]
    inner = grad_ext[:, rim_rows : rim_rows + patches_per_part]
    from_next = passed_along(before_rim.astype(jnp.bfloat16), "grid", -1).astype(before_rim.dtype)
    from_prev = passed_along(after_rim.astype(jnp.bfloat16), "grid", 1).astype(after_rim.dtype)
    inner = inner.at[:, :rim_rows].add(from_prev)
    inner = inner.at[:, patches_per_part - rim_rows :].add(from_next)
    grad_proj = jnp.concatenate(
        [grad_queries.reshape(members_per_part, patches_per_part, model_width), inner], axis=-1
    ).astype(jnp.bfloat16)
    value_part = jnp.einsum(
        "mpd,mpe->de",
        normed,
        grad_proj[:, :, 2 * model_width :],
        preferred_element_type=jnp.float32,
    )
    grad_normed = jnp.einsum(
        "mpe,de->mpd", grad_proj, attention_matrix, preferred_element_type=jnp.float32
    )
    unit_input = lat_float * inv_first
    embedding_sensitivity = grad_state + inv_first * (
        grad_normed - unit_input * jnp.mean(grad_normed * unit_input, axis=-1, keepdims=True)
    )
    flat_value = value_part.reshape(-1)
    flat_dec = grad_dec_part.reshape(-1)
    grad_value_matrix, grad_dec = (
        lax.psum_scatter(flat_value, ("ens", "grid"), scatter_dimension=0, tiled=True),
        lax.psum_scatter(flat_dec, ("ens", "grid"), scatter_dimension=0, tiled=True),
    )
    return (energy_objective, embedding_sensitivity, grad_value_matrix, grad_dec)


def solution(mesh):
    in_specs = (
        P("ens", "grid", None),
        P(None, "grid"),
        P(),
        P(),
        P("grid", None),
        P(),
        P("grid"),
        P("grid"),
    )
    out_specs = (P(), P("ens", "grid", None), P(("ens", "grid")), P(("ens", "grid")))
    return jax.shard_map(
        per_device, mesh=mesh, in_specs=in_specs, out_specs=out_specs, check_vma=False
    )
```

profile of v0, /device:TPU:16, one launch (start us, length us, event | category | flops | bytes accessed | tf_op | source)
XLA Modules:
  0.0 441.0 jit_solution(3811326768805656858)
XLA Ops:
  7.2 1.3 fusion.60
  8.5 1.2 fusion.52
  9.7 3.3 collective-permute-start.1
  13.0 2.5 collective-permute-start
  15.6 0.7 compare_and_fusion
  16.3 0.7 subtract_add_fusion
  17.0 4.6 %fusion.15 = bf16[2,128,3072]{2,1,0:T(8,128)(2,1)S(1)} fusion(bf16[2,128,1024]{2,1,0:T(8,128)(2,1)S(1)} %fusion.52, bf16[1024,3072]{1,0:T(8,128)(2,1)} %param.18), kind=kOutput, calls=%fused_computation.19 | convolution fusion | flops 1611399168 | bytes 8388608 | tf_op jit(solution)/shard_map/mpd,de->mpe/dot_general | solution.py:66
  21.7 1.1 slice.88
  23.5 0.7 reshape.367
  24.1 2.0 copy.87
  26.3 10.3 %collective-permute-done.1 = bf16[2,128,1024]{2,1,0:T(8,128)(2,1)S(1)} collective-permute-done((bf16[2,128,1024]{2,1,0:T(8,128)(2,1)S(1)}, bf16[2,128,1024]{2,1,0:T(8,128)(2,1)S(1)}, u32[]{:S(2)}, u32[]{:S(2)}) %collective-permute-start.1) | collective-permute-done | bytes 524320 | tf_op jit(solution)/shard_map/ppermute | solution.py:27
  36.5 4.5 %fusion.23 = bf16[2,256,2048]{2,1,0:T(8,128)(2,1)S(1)} fusion(bf16[1024,3072]{1,0:T(8,128)(2,1)} %param.18, bf16[2,128,1024]{2,1,0:T(8,128)(2,1)S(1)} %collective-permute-done.1, bf16[2,128,1024]{2,1,0:T(8,128)(2,1)S(1)} %collective-permute-done), kind=kOutput, calls=%fused_computation.23 | convolution fusion | flops 2150629376 | bytes 7340032 | tf_op jit(solution)/shard_map/mpd,de->mpe/dot_general | solution.py:75
  41.2 1.1 copy-done.7
  42.5 2.5 gather_fusion
  45.0 2.1 copy.76
  47.2 7.7 %gather.7 = bf16[2,2,192,2,16,64]{5,4,3,2,1,0:T(8,128)(2,1)} reshape(bf16[2,6,64,2048]{3,2,1,0:T(8,128)(2,1)S(1)} %copy.76) | data formatting | bytes 6291456 | tf_op jit(solution)/shard_map/jit(_take)/gather | solution.py:87
  54.8 9.1 %copy.77 = bf16[2,2,192,2,16,64]{2,5,4,1,0,3:T(8,128)(2,1)} copy(bf16[2,2,192,2,16,64]{5,4,3,2,1,0:T(8,128)(2,1)} %gather.7) | data formatting | bytes 6291456 | tf_op jit(solution)/shard_map/jit(_take)/gather | solution.py:87
  63.9 2.6 broadcast_select_fusion
  66.6 0.8 fusion.42
  67.4 3.3 fusion.111
  71.1 12.6 %fusion.43 = f32[2,2,64,16,64]{2,4,3,1,0:T(8,128)} fusion(bf16[2,2,192,2,16,64]{2,5,4,1,0,3:T(8,128)(2,1)} %copy-done.4, f32[2,2,16,64]{3,2,1,0:T(8,128)S(1)} %get-tuple-element.56, f32[2,2,16,64,192]{4,3,2,1,0:T(8,128)} %copy-done.5), kind=kOutput, calls=%fused_computation.41 | convolution fusion | flops 104599744 | bytes 11550720 | tf_op jit(solution)/shard_map/mbhqk,mbkhe->mbqhe/dot_general | solution.py:103
  83.8 3.1 copy.79
  86.9 2.5 reshape.368
  89.6 0.5 fusion.74
  90.1 6.6 %all_gather.3 = f32[8,100,128]{2,1,0:T(8,128)S(1)} all-gather(f32[2,100,128]{2,1,0:T(8,128)S(1)} %bitcast.133), channel_id=1, replica_groups=mesh['ens'=4,'grid'=8] {'ens'}, dimensions={0}, use_global_device_ids=true | all-gather | bytes 512000 | tf_op jit(solution)/shard_map/all_gather | solution.py:116
  96.7 0.5 fusion.67
  97.4 0.6 add_sqrt_fusion
  98.1 0.8 fusion.81
  98.9 0.8 copy.117
  99.9 0.6 add_sqrt_fusion.1
  100.5 21.2 %reduce-scatter.2.cloned.1.call-done = f32[2,100,1,128]{3,1,0,2:T(8,128)} async-done(((f32[8,100,1,128]{3,1,0,2:T(8,128)}), f32[2,100,1,128]{3,1,0,2:T(8,128)}) %reduce-scatter.2.cloned.1.call-update) | async-done | bytes 102416 | tf_op jit(solution)/shard_map/reduce_scatter | solution.py:160
  121.8 1.0 fusion.83
  123.5 1.6 reshape.371
  125.2 2.8 copy.88
  127.9 13.0 %convolution_bitcast_fusion = f32[2,2,192,1,16,64]{2,5,4,1,0,3:T(8,128)} fusion(bf16[2,2,64,16,64]{2,4,3,1,0:T(8,128)(2,1)} %copy.88, f32[2,2,16,64]{3,2,1,0:T(8,128)S(1)} %get-tuple-element.56, f32[2,2,16,64,192]{4,3,2,1,0:T(8,128)} %copy-done.5), kind=kOutput, calls=%fused_computation.26 | convolution fusion | flops 104599744 | bytes 6832128 | tf_op jit(solution)/shard_map/mbhqk,mbqhe->mbkhe/dot_general | solution.py:190
  140.9 4.6 %fusion.40 = f32[2,2,16,64,192]{4,3,2,1,0:T(8,128)} fusion(bf16[2,2,64,16,64]{2,4,3,1,0:T(8,128)(2,1)} %copy.88, bf16[2,2,192,2,16,64]{2,5,4,1,0,3:T(8,128)(2,1)} %copy-done.4), kind=kOutput, calls=%fused_computation.38 | convolution fusion | flops 100663296 | bytes 6291456 | tf_op jit(solution)/shard_map/mbqhe,mbkhe->mbhqk/dot_general | solution.py:187
  145.5 30.9 %fusion.32 = f32[2,2,192,1,16,64]{2,5,4,1,0,3:T(8,128)} fusion(bf16[2,2,64,16,64]{2,4,3,1,0:T(8,128)(2,1)} %copy.87, f32[2,2,16,64,192]{4,3,2,1,0:T(8,128)} %fusion.40, f32[2,2,16,64,192]{4,3,2,1,0:T(8,128)} %get-tuple-element.57, f32[2,2,16,64]{3,2,1,0:T(8,128)S(1)} %get-tuple-element.56), kind=kOutput, calls=%fused_computation.27 | convolution fusion | flops 106172608 | bytes 9977856 | tf_op jit(solution)/shard_map/mbhqk,mbqhe->mbkhe/dot_general | solution.py:201
  176.4 8.0 %pad_maximum_fusion = f32[2,2,192,2,16,64]{2,5,4,1,0,3:T(8,128)} fusion(f32[2,2,192,1,16,64]{2,5,4,1,0,3:T(8,128)} %convolution_bitcast_fusion, f32[2,2,192,1,16,64]{2,5,4,1,0,3:T(8,128)} %fusion.32), kind=kLoop, calls=%fused_computation.3 | loop fusion | flops 1572864 | bytes 12582912 | tf_op jit(solution)/shard_map/stack | solution.py:204
  184.4 12.2 %copy.89 = f32[2,2,192,2,16,64]{5,4,3,2,1,0:T(8,128)} copy(f32[2,2,192,2,16,64]{2,5,4,1,0,3:T(8,128)} %pad_maximum_fusion) | data formatting | bytes 12582912 | tf_op jit(solution)/shard_map/stack | solution.py:204
  196.6 11.9 %reshape.373 = f32[2,6,64,2048]{3,2,1,0:T(8,128)} reshape(f32[2,2,192,2,16,64]{5,4,3,2,1,0:T(8,128)} %copy.89) | data formatting | bytes 12582912 | tf_op jit(solution)/shard_map/reshape | solution.py:204
  208.5 12.0 %fusion.8 = f32[2,6,64,2048]{3,1,2,0:T(8,128)S(1)} fusion(f32[2,6,64,2048]{3,2,1,0:T(8,128)} %reshape.373, s32[6]{0:T(128)S(1)} %reshape.374), kind=kOutput, calls=%fused_computation.10 | convolution fusion | flops 113246240 | bytes 12582936 | tf_op jit(solution)/shard_map/sn,msqc->mnqc/dot_general | solution.py:210
  220.6 3.6 copy.91
  224.2 0.5 bitcast_convert_fusion
  224.7 2.2 copy-done.2
  226.9 1.6 fusion.109
  228.4 3.5 collective-permute-start.2
  231.9 3.6 collective-permute-start.3
  235.5 1.2 convolution_bitcast_fusion.2
  236.7 2.5 reshape.377
  239.2 37.9 %collective-permute-done.2 = bf16[2,128,2048]{2,1,0:T(8,128)(2,1)} collective-permute-done((bf16[2,128,2048]{2,1,0:T(8,128)(2,1)}, bf16[2,128,2048]{2,1,0:T(8,128)(2,1)}, u32[]{:S(2)}, u32[]{:S(2)}) %collective-permute-start.2) | collective-permute-done | bytes 1048608 | tf_op jit(solution)/shard_map/ppermute | solution.py:35
  277.1 1.9 collective-permute-done.3
  279.0 2.6 fusion.36
  281.6 1.0 copy-done.10
  282.6 0.8 convolution_bitcast_fusion.1
  283.3 3.0 copy.98
  287.6 39.7 %psum.7 = f32[]{:T(128)} all-reduce(f32[]{:T(128)S(6)} %sub.58), channel_id=1, replica_groups=mesh['ens'=4,'grid'=8] {'ens','grid'}, use_global_device_ids=true, to_apply=%region_10.11 | all-reduce | flops 1 | bytes 8 | tf_op jit(solution)/shard_map/psum | solution.py:164
  328.0 29.5 %fusion.53 = bf16[2,2,64,16,64]{2,4,3,1,0:T(8,128)(2,1)} fusion(f32[2,2,16,64,192]{4,3,2,1,0:T(8,128)} %fusion.40, bf16[2,2,192,2,16,64]{2,5,4,1,0,3:T(8,128)(2,1)} %copy-done.4, f32[2,2,16,64,192]{4,3,2,1,0:T(8,128)} %get-tuple-element.57, f32[2,2,16,64]{3,2,1,0:T(8,128)S(1)} %get-tuple-element.56), kind=kOutput, calls=%fused_computation.52 | convolution fusion | flops 106434752 | bytes 19464192 | tf_op jit(solution)/shard_map/mbhqk,mbkhe->mbqhe/dot_general | solution.py:198
  357.5 2.6 copy.86
  360.2 1.9 reshape.372
  362.1 5.2 %fusion.56 = (f32[2,128]{1,0:T(2,128)S(1)}, f32[2,128,1024]{2,1,0:T(8,128)S(1)}) fusion(bf16[2,128,1024]{2,1,0:T(8,128)(2,1)S(1)} %copy-done.3, f32[2,128]{1,0:T(2,128)S(1)} %add_rsqrt_fusion.1, bf16[1024,3072]{1,0:T(8,128)(2,1)} %param.18, bf16[2,128,2048]{2,1,0:T(8,128)(2,1)} %copy-done.10, bf16[2,128,1024]{2,1,0:T(8,128)(2,1)S(1)} %reshape.372), kind=kOutput, calls=%fused_computation.54 | convolution fusion | flops 1614806784 | bytes 9439232 | tf_op jit(solution)/shard_map/mpe,de->mpd/dot_general | solution.py:229
  367.3 1.4 fusion.59
  368.8 61.0 %all-reduce.5.cloned.1.call-done = (f32[1048576]{0:T(1024)}, f32[102400]{0:T(1024)}) async-done(((f32[1048576]{0:T(1024)}, f32[102400]{0:T(1024)}), (f32[1048576]{0:T(1024)}, f32[102400]{0:T(1024)})) %all-reduce.5.cloned.1.call-update) | async-done | bytes 4603920
  429.8 1.6 dynamic-slice.10
  431.3 1.4 dynamic-slice.11
  (59 shorter events, 3.2 us)
Async XLA Ops:
  7.2 82.4 %copy-start = (bf16[1024,100]{0,1:T(8,128)(2,1)S(1)}, bf16[1024,100]{0,1:T(8,128)(2,1)}, u32[]{:S(2)}) copy-start(bf16[1024,100]{0,1:T(8,128)(2,1)} %param.19) | copy-start | bytes 614404
  7.2 114.6 %reduce-scatter.2.cloned.1.call-start = ((), (), s32[]{:S(2)}) async-start(), calls=%async_computation.1 | async-start | bytes 532480 | tf_op jit(solution)/shard_map/reduce_scatter | solution.py:160
  9.7 11.9 %copy-start.8 = (bf16[2,128,1024]{2,1,0:T(8,128)(2,1)}, bf16[2,128,1024]{2,1,0:T(8,128)(2,1)S(1)}, u32[]{:S(2)}) copy-start(bf16[2,128,1024]{2,1,0:T(8,128)(2,1)S(1)} %fusion.52) | copy-start | bytes 1572868
  9.7 26.8 %collective-permute-start.1 = (bf16[2,128,1024]{2,1,0:T(8,128)(2,1)S(1)}, bf16[2,128,1024]{2,1,0:T(8,128)(2,1)S(1)}, u32[]{:S(2)}, u32[]{:S(2)}) collective-permute-start(bf16[2,128,1024]{2,1,0:T(8,128)(2,1)S(1)} %fusion.52), channel_id=1, source_target_pairs={{1,0},{2,1},{3,2},{4,3},{5,4},{6,5},{7,6},{9,8},{10,9},{11,10},{12... | collective-permute-start | bytes 1572872 | tf_op jit(solution)/shard_map/ppermute | solution.py:27
  13.0 23.5 %collective-permute-start = (bf16[2,128,1024]{2,1,0:T(8,128)(2,1)S(1)}, bf16[2,128,1024]{2,1,0:T(8,128)(2,1)S(1)}, u32[]{:S(2)}, u32[]{:S(2)}) collective-permute-start(bf16[2,128,1024]{2,1,0:T(8,128)(2,1)S(1)} %fusion.52), channel_id=1, source_target_pairs={{0,1},{1,2},{2,3},{3,4},{4,5},{5,6},{6,7},{8,9},{9,10},{10,11},{11... | collective-permute-start | bytes 1572872 | tf_op jit(solution)/shard_map/ppermute | solution.py:26
  17.0 6.1 %copy-start.12 = (s32[7,8]{1,0:T(8,128)S(1)}, s32[7,8]{1,0:T(8,128)}, u32[]{:S(2)}) copy-start(s32[7,8]{1,0:T(8,128)} %param.21) | copy-start | bytes 676
  21.6 4.5 %copy-start.13 = (s32[128]{0:T(128)S(1)}, s32[128]{0:T(128)}, u32[]{:S(2)}) copy-start(s32[128]{0:T(128)} %param.22) | copy-start | bytes 1540
  21.6 4.5 %copy-start.14 = (s32[128]{0:T(128)S(1)}, s32[128]{0:T(128)}, u32[]{:S(2)}) copy-start(s32[128]{0:T(128)} %param.23) | copy-start | bytes 1540
  41.0 1.2 copy-start.7
  63.9 2.7 copy-start.6
  66.6 4.1 copy-start.4
  67.4 3.8 copy-start.5
  83.8 5.6 %copy-start.3 = (bf16[2,128,1024]{2,1,0:T(8,128)(2,1)S(1)}, bf16[2,128,1024]{2,1,0:T(8,128)(2,1)}, u32[]{:S(2)}) copy-start(bf16[2,128,1024]{2,1,0:T(8,128)(2,1)} %param.16) | copy-start | bytes 1572868
  83.8 5.8 %copy-start.11 = (f32[100,128]{1,0:T(8,128)S(1)}, f32[100,128]{1,0:T(8,128)}, u32[]{:S(2)}) copy-start(f32[100,128]{1,0:T(8,128)} %param.17) | copy-start | bytes 153604
  99.8 330.0 %all-reduce.5.cloned.1.call-start = ((), (), s32[]{:S(2)}) async-start(), calls=%async_computation.2 | async-start | bytes 9207808
  224.2 2.7 copy-start.2
  228.4 54.2 %copy-start.9 = (bf16[2,128,1024]{2,1,0:T(8,128)(2,1)S(1)}, bf16[2,128,1024]{2,1,0:T(8,128)(2,1)}, u32[]{:S(2)}) copy-start(bf16[2,128,1024]{2,1,0:T(8,128)(2,1)} %copy-done.8) | copy-start | bytes 1572868
  228.4 48.7 %collective-permute-start.2 = (bf16[2,128,2048]{2,1,0:T(8,128)(2,1)}, bf16[2,128,2048]{2,1,0:T(8,128)(2,1)}, u32[]{:S(2)}, u32[]{:S(2)}) collective-permute-start(bf16[2,128,2048]{2,1,0:T(8,128)(2,1)} %get-tuple-element.48), channel_id=1, source_target_pairs={{0,1},{1,2},{2,3},{3,4},{4,5},{5,6},{6,7},{8,9},{9,10},{10,11},{11... | collective-permute-start | bytes 3145736 | tf_op jit(solution)/shard_map/ppermute | solution.py:35
  231.9 47.1 %collective-permute-start.3 = (bf16[2,128,2048]{2,1,0:T(8,128)(2,1)}, bf16[2,128,2048]{2,1,0:T(8,128)(2,1)}, u32[]{:S(2)}, u32[]{:S(2)}) collective-permute-start(bf16[2,128,2048]{2,1,0:T(8,128)(2,1)} %get-tuple-element.49), channel_id=1, source_target_pairs={{1,0},{2,1},{3,2},{4,3},{5,4},{6,5},{7,6},{9,8},{10,9},{11,10},{12... | collective-permute-start | bytes 3145736 | tf_op jit(solution)/shard_map/ppermute | solution.py:35
  281.6 1.0 copy-start.10
  362.1 70.6 %copy-start.1 = (bf16[1024,100]{0,1:T(8,128)(2,1)S(1)}, bf16[1024,100]{0,1:T(8,128)(2,1)}, u32[]{:S(2)}) copy-start(bf16[1024,100]{0,1:T(8,128)(2,1)} %param.19) | copy-start | bytes 614404
Sparse Core Ops, SparseCore 0:
  99.9 21.8 reduce-scatter.1
  286.5 143.2 all-reduce.4
where the time goes:
time: 447 us; the launch traced here: 441 us
  waiting for transfers between devices  132 us (30%)
  matrix products  122 us (27%)
  local copies, waits for them, and re-layouts  83.5 us (19%)
  blocking collectives  46.3 us (10%)
  other arithmetic  26.1 us (6%)
  between operations  17.7 us (4%)
  starting transfers between devices  13 us (3%)
    unnamed x3, waiting for transfers between devices  61 us
    ppermute x2, waiting for transfers between devices, passed_along(): lax.ppermute(value, axis, [(source, source + steps) for source in range(l...  39.8 us
    psum x1, blocking collectives, per_device(): total = lax.psum(local_total, ('ens', 'grid'))  39.7 us
    dot_general x1, matrix products, per_device(): jnp.einsum('mbhqk,mbqhe->mbkhe', grad_scores, query_blocks, preferred_ele...  30.9 us
    dot_general x1, matrix products, per_device(): jnp.einsum('mbhqk,mbkhe->mbqhe', grad_scores, window_keys, preferred_elem...  29.5 us
    gather x4, local copies, waits for them, and re-layouts, per_device(): jnp.take(ext_view, local_slots, axis=1)  21.4 us
    reduce_scatter x1, waiting for transfers between devices, per_device(): lax.psum_scatter(outgoing, 'ens', scatter_dimension=0, tiled=True)  21.2 us
    dot_general x1, matrix products, per_device(): jnp.einsum('mbhqk,mbqhe->mbkhe', attention16, grad_out16, preferred_eleme...  13 us
  transfers between devices with their start and end apart: 6, of which 5 were waited for; matrix products, arithmetic and copies ran while one was open for 13% of the time, Pallas kernels for 0%

commit v1 on v0

v1 whole, which is shorter than its diff:
```python
import functools
import math

import jax
import jax.numpy as jnp
from jax import lax
from jax.experimental import pallas as pl
from jax.experimental.pallas import tpu as pltpu
from jax.sharding import PartitionSpec as P

HEADS = 16
QB = 64
R_BLK = 2
NB = 3
SCORED_ENTRIES = 128
NLAT = 721
EPSILON = 1e-06
RIM = R_BLK * QB
LANES = 128
NEG = -1e30

F32 = jnp.float32
BF16 = jnp.bfloat16
MESH = pl.DeviceIdType.MESH


def mm(a, b):
    return lax.dot_general(a, b, (((1,), (0,)), ((), ())), preferred_element_type=F32)


def mm_nt(a, b):
    return lax.dot_general(a, b, (((1,), (1,)), ((), ())), preferred_element_type=F32)


def mm_tn(a, b):
    return lax.dot_general(a, b, (((0,), (0,)), ((), ())), preferred_element_type=F32)


def rms_scale(values):
    return lax.rsqrt(jnp.mean(values * values, axis=-1, keepdims=True) + EPSILON)


def kernel(
    n_ens, n_grid, channels,
    adj_ref, comp_ref, x_ref, ref_ref, w_ref, r_ref, weight_ref,
    tot_ref, out_ref, gv_ref, gd_ref,
    nrm, q_s, kv, cnt_s, ac_s, state, hid, go, gq, gkv, fc,
    vp, rc0, s1, rc1, s2, r2, gnr, gnx, tq, tg,
    halo_send, halo_recv, fc_send, fc_recv, core_send, core_recv,
    x_send, x_recv, g_send, g_recv, back_send, back_recv,
    tq_send, tq_recv, tg_send, tg_recv,
):
    members, points, width = x_ref.shape
    ext = points + 2 * RIM
    nblk = points // QB
    pairs = width // LANES
    rounds = comp_ref.shape[0]
    patches = points // SCORED_ENTRIES
    rows_pp = width // (n_ens * n_grid)
    fold = max(1, 16 // rows_pp)
    wide = width // fold
    n_far = n_ens // 2
    e = lax.axis_index("ens")
    g = lax.axis_index("grid")
    core = e % 2
    far = e // 2
    scale = 1.0 / math.sqrt(width // HEADS)

    def ens_copy(src, dst, ss, rs, to):
        return pltpu.make_async_remote_copy(
            src_ref=src, dst_ref=dst, send_sem=ss, recv_sem=rs,
            device_id={"ens": to}, device_id_type=MESH,
        )

    def grid_copy(src, dst, ss, rs, to):
        return pltpu.make_async_remote_copy(
            src_ref=src, dst_ref=dst, send_sem=ss, recv_sem=rs,
            device_id={"grid": to}, device_id_type=MESH,
        )

    for m in range(members):
        lat = x_ref[m].astype(F32)
        nrm[m, RIM : RIM + points] = (lat * rms_scale(lat)).astype(BF16)

    @pl.when(g == 0)
    def _():
        nrm[:, :RIM] = jnp.zeros((members, RIM, width), BF16)

    @pl.when(g == n_grid - 1)
    def _():
        nrm[:, RIM + points :] = jnp.zeros((members, RIM, width), BF16)

    barrier = pltpu.get_barrier_semaphore()
    for k in range(1, n_ens):
        pl.semaphore_signal(barrier, inc=1, device_id={"ens": (e + k) % n_ens}, device_id_type=MESH)
    for k in range(1, n_grid):
        pl.semaphore_signal(barrier, inc=1, device_id={"grid": (g + k) % n_grid}, device_id_type=MESH)
    pl.semaphore_wait(barrier, n_ens + n_grid - 2)

    up = grid_copy(nrm.at[:, pl.ds(points, RIM)], nrm.at[:, pl.ds(0, RIM)],
                   halo_send.at[0], halo_recv.at[0], (g + 1) % n_grid)
    down = grid_copy(nrm.at[:, pl.ds(RIM, RIM)], nrm.at[:, pl.ds(RIM + points, RIM)],
                     halo_send.at[1], halo_recv.at[1], (g + n_grid - 1) % n_grid)

    @pl.when(g < n_grid - 1)
    def _():
        up.start()

    @pl.when(g > 0)
    def _():
        down.start()

    tile = 512

    @pl.loop(0, width // tile)
    def _(t):
        own = nrm[:, RIM : RIM + points].reshape(members * points, width)
        c = pl.multiple_of(t * tile, tile)
        q_s[:, :, pl.ds(c, tile)] = mm(own, w_ref[:, pl.ds(c, tile)]).astype(BF16).reshape(
            members, points, tile
        )

    @pl.loop(0, 2 * width // tile)
    def _(t):
        own = nrm[:, RIM : RIM + points].reshape(members * points, width)
        c = pl.multiple_of(t * tile, tile)
        wt = w_ref[:, pl.ds(pl.multiple_of(c + width, tile), tile)]
        kv[:, RIM : RIM + points, pl.ds(c, tile)] = mm(own, wt).astype(BF16).reshape(
            members, points, tile
        )

    col = lax.broadcasted_iota(jnp.int32, (1, ext), 1)
    for b in range(nblk):
        count = jnp.zeros((1, ext), F32)
        for n in range(NB):
            first = (adj_ref[b, n] - g * nblk + R_BLK) * QB
            count += jnp.where((col >= first) & (col < first + QB), 1.0, 0.0)
        rows = jnp.broadcast_to(count, (QB, ext))
        cnt_s[b * QB : (b + 1) * QB] = rows
        cnt_s[points + b * QB : points + (b + 1) * QB] = rows

    @pl.when(g > 0)
    def _():
        up.wait_recv()

    @pl.when(g < n_grid - 1)
    def _():
        down.wait_recv()

    @pl.loop(0, 2 * width // tile)
    def _(t):
        c = pl.multiple_of(t * tile, tile)
        wt = w_ref[:, pl.ds(pl.multiple_of(c + width, tile), tile)]
        rim = jnp.concatenate(
            [nrm[:, :RIM].reshape(members * RIM, width),
             nrm[:, RIM + points :].reshape(members * RIM, width)], axis=0
        )
        res = mm(rim, wt).astype(BF16)
        kv[:, :RIM, pl.ds(c, tile)] = res[: members * RIM].reshape(members, RIM, tile)
        kv[:, RIM + points :, pl.ds(c, tile)] = res[members * RIM :].reshape(members, RIM, tile)

    head_a = lax.broadcasted_iota(jnp.int32, (points, LANES), 1) < LANES // 2

    def stacked(v):
        zero = jnp.zeros_like(v)
        return jnp.concatenate([jnp.where(head_a, v, zero), jnp.where(head_a, zero, v)], axis=0)

    def merged(v):
        return jnp.where(head_a, v[:points], v[points:])

    def place(it):
        m = it // pairs
        c = pl.multiple_of((it % pairs) * LANES, LANES)
        return m, pl.ds(c, LANES), pl.ds(pl.multiple_of(c + width, LANES), LANES)

    @pl.loop(0, members * pairs)
    def _(it):
        m, ck, cv = place(it)
        s = mm_nt(stacked(q_s[m, :, ck]), kv[m, :, ck]) * scale
        cnt = cnt_s[...]
        s = jnp.where(cnt > 0.0, s, NEG)
        ex = jnp.exp(s - jnp.max(s, axis=-1, keepdims=True)) * cnt
        a = ex * (1.0 / jnp.sum(ex, axis=-1, keepdims=True))
        ac_s[it] = a
        state[m, :, ck] = merged(mm(a.astype(BF16), kv[m, :, cv]))

    for m in range(members):
        st = x_ref[m].astype(F32) + state[m]
        state[m] = st
        h = (st * rms_scale(st)).astype(BF16)
        hid[m * points : (m + 1) * points] = h
        fc[e, m] = mm(h, r_ref[...])

    fcs = []
    for k in range(1, n_ens):
        cp = ens_copy(fc.at[e], fc.at[e], fc_send.at[k], fc_recv.at[k], (e + k) % n_ens)
        cp.start()
        fcs.append(cp)
    for cp in fcs:
        cp.wait()

    lane = lax.broadcasted_iota(jnp.int32, (1, LANES), 1)
    valid = lane < channels
    total = jnp.zeros((1, LANES), F32)
    g16 = []
    for m in range(members):
        parts = []
        for j in range(patches):
            rows = slice(j * SCORED_ENTRIES, (j + 1) * SCORED_ENTRIES)
            rnd = (lane + g * patches + j) % rounds
            partner = jnp.zeros((1, LANES), jnp.int32)
            for r in range(rounds):
                partner = jnp.where(rnd == r, comp_ref[r, e * members + m], partner)
            f = fc[e, m, rows]
            pf = jnp.zeros_like(f)
            for n in range(n_ens * members):
                pf = jnp.where(partner == n, fc[n // members, n % members, rows], pf)
            wgt = weight_ref[rows]
            err = f - ref_ref[rows]
            dif = f - pf
            dt = jnp.sqrt(jnp.sum(wgt * err * err, axis=0, keepdims=True) + EPSILON)
            dp = jnp.sqrt(jnp.sum(wgt * dif * dif, axis=0, keepdims=True) + EPSILON)
            total += jnp.where(valid, dt - 0.5 * dp, 0.0)
            parts.append((wgt * err / dt - wgt * dif / dp).astype(BF16))
        g16.append(jnp.concatenate(parts, axis=0) if patches > 1 else parts[0])
    g_all = jnp.concatenate(g16, axis=0)

    tq[e] = jnp.broadcast_to(jnp.sum(total, axis=-1, keepdims=True), (8, LANES))
    tqs = []
    for k in range(1, n_ens):
        cp = ens_copy(tq.at[e], tq.at[e], tq_send.at[k], tq_recv.at[k], (e + k) % n_ens)
        cp.start()
        tqs.append(cp)

    for m in range(members):
        gh = mm_nt(g16[m], r_ref[...])
        st = state[m]
        inv = rms_scale(st)
        y = st * inv
        gs = inv * (gh - y * jnp.mean(gh * y, axis=-1, keepdims=True))
        out_ref[m] = gs
        go[m] = gs.astype(BF16)

    @pl.loop(0, members * pairs)
    def _(it):
        m, ck, cv = place(it)
        gkv[m, :, cv] = mm_tn(ac_s[it].astype(BF16), stacked(go[m, :, ck])).astype(BF16)

    per_ens = width // n_ens

    def folded(v, cols):
        v = v.reshape(n_grid, rows_pp, cols)
        if fold > 1:
            step = cols // fold
            v = jnp.concatenate([v[:, :, i * step : (i + 1) * step] for i in range(fold)], axis=1)
        return v.astype(BF16)

    @pl.loop(0, n_ens)
    def _(qd):
        d = pl.ds(pl.multiple_of(qd * per_ens, per_ens), per_ens)
        acc = jnp.zeros((per_ens, width), F32)
        for m in range(members):
            acc += mm_tn(nrm[m, :, d], gkv[m, :, width:])
        vp[qd, :, :, :wide] = folded(acc, width)
        dec = mm_tn(hid[:, d], g_all)
        if fold > 1:
            dec = jnp.concatenate(
                [dec, jnp.zeros((per_ens, LANES * (fold - 1)), F32)], axis=1
            )
        vp[qd, :, :, wide:] = folded(dec, LANES * fold)

    cores = []
    for k in range(n_far):
        f = (far + 1 + k) % n_far
        cp = ens_copy(vp.at[2 * f + 1 - core], rc0.at[f], core_send.at[k], core_recv.at[k],
                      2 * far + 1 - core)
        cp.start()
        cores.append(cp)

    for cp in tqs:
        cp.wait()
    tg[g] = functools.reduce(lambda a, b: a + b, [tq[i] for i in range(n_ens)])
    tgs = []
    for k in range(1, n_grid):
        cp = grid_copy(tg.at[g], tg.at[g], tg_send.at[k], tg_recv.at[k], (g + k) % n_grid)
        cp.start()
        tgs.append(cp)

    def back(it):
        m, ck, cv = place(it)
        a = ac_s[it]
        da = mm_nt(stacked(go[m, :, ck]), kv[m, :, cv])
        ds = a * (da - jnp.sum(a * da, axis=-1, keepdims=True)) * scale
        ds = ds.astype(BF16)
        gq[m, :, ck] = merged(mm(ds, kv[m, :, ck])).astype(BF16)
        gkv[m, :, ck] = mm_tn(ds, stacked(q_s[m, :, ck])).astype(BF16)

    split = 2

    @pl.loop(0, split)
    def _(it):
        back(it)

    xs = []
    for k in range(n_far - 1):
        cores[k].wait()
        f = (far + 1 + k) % n_far
        s1[k] = (vp[2 * f + core].astype(F32) + rc0[f].astype(F32)).astype(BF16)
        cp = ens_copy(s1.at[k], rc1.at[k], x_send.at[k], x_recv.at[k], 2 * f + core)
        cp.start()
        xs.append(cp)
    cores[n_far - 1].wait()

    @pl.loop(split, members * pairs)
    def _(it):
        back(it)

    dt_tile = 256

    @pl.loop(0, width // dt_tile)
    def _(t):
        d = pl.ds(pl.multiple_of(t * dt_tile, dt_tile), dt_tile)
        rim = jnp.concatenate(
            [gkv[:, :RIM].reshape(members * RIM, 2 * width),
             gkv[:, RIM + points :].reshape(members * RIM, 2 * width)], axis=0
        )
        res = mm_nt(rim, w_ref[d, width:]).astype(BF16)
        gnr[:, :, :, d] = res.reshape(2, members, RIM, dt_tile)

    to_prev = grid_copy(gnr.at[0], gnx.at[0], back_send.at[0], back_recv.at[0],
                        (g + n_grid - 1) % n_grid)
    to_next = grid_copy(gnr.at[1], gnx.at[1], back_send.at[1], back_recv.at[1], (g + 1) % n_grid)

    @pl.when(g > 0)
    def _():
        to_prev.start()

    @pl.when(g < n_grid - 1)
    def _():
        to_next.start()

    for cp in xs:
        cp.wait()
    part = vp[2 * far + core].astype(F32) + rc0[far].astype(F32)
    for k in range(n_far - 1):
        part += rc1[k].astype(F32)
    s2[...] = part.astype(BF16)
    gcs = []
    for k in range(1, n_grid):
        to = (g + k) % n_grid
        cp = grid_copy(s2.at[to], r2.at[k], g_send.at[k], g_recv.at[k], to)
        cp.start()
        gcs.append(cp)

    @pl.loop(0, width // dt_tile)
    def _(t):
        d = pl.ds(pl.multiple_of(t * dt_tile, dt_tile), dt_tile)
        res = mm_nt(gq[...].reshape(members * points, width), w_ref[d, :width])
        res += mm_nt(gkv[:, RIM : RIM + points].reshape(members * points, 2 * width),
                     w_ref[d, width:])
        state[:, :, d] = res.reshape(members, points, dt_tile)

    @pl.when(g < n_grid - 1)
    def _():
        to_prev.wait_recv()
        state[:, points - RIM :] += gnx[0].astype(F32)

    @pl.when(g > 0)
    def _():
        to_next.wait_recv()
        state[:, :RIM] += gnx[1].astype(F32)

    for m in range(members):
        lat = x_ref[m].astype(F32)
        inv = rms_scale(lat)
        y = lat * inv
        gn = state[m]
        out_ref[m] += inv * (gn - y * jnp.mean(gn * y, axis=-1, keepdims=True))

    for cp in tgs:
        cp.wait()
    tot_ref[...] = functools.reduce(lambda a, b: a + b, [tg[i] for i in range(n_grid)])

    for cp in gcs:
        cp.wait()
    acc = s2[g].astype(F32)
    for k in range(1, n_grid):
        acc += r2[k].astype(F32)
    for i in range(fold):
        gv_ref[:, i * wide : (i + 1) * wide] = acc[i * rows_pp : (i + 1) * rows_pp, :wide]
    gd_ref[...] = acc[:rows_pp, wide:]

    @pl.when(g < n_grid - 1)
    def _():
        up.wait_send()
        to_next.wait_send()

    @pl.when(g > 0)
    def _():
        down.wait_send()
        to_prev.wait_send()


def per_device(
    embeddings,
    reference_analysis,
    attention_matrix,
    readout_matrix,
    adjacent_blocks,
    companion_matrix,
    continent_indicator,
    zonal_strip,
):
    members, points, width = embeddings.shape
    channels = reference_analysis.shape[0]
    n_ens, n_grid = lax.axis_size("ens"), lax.axis_size("grid")
    ext = points + 2 * RIM
    pairs = width // LANES
    rows_pp = width // (n_ens * n_grid)
    fold = max(1, 16 // rows_pp)
    chunk = (rows_pp * fold, width // fold + LANES)
    n_far = n_ens // 2
    phase = (zonal_strip.astype(F32) + 0.5) * (math.pi / NLAT) - 0.5 * math.pi
    weight = (jnp.cos(phase) * (1.0 + continent_indicator.astype(F32)))[:, None]
    target = jnp.pad(reference_analysis.T, ((0, 0), (0, LANES - channels)))
    readout = jnp.pad(readout_matrix, ((0, 0), (0, LANES - channels)))
    vmem = pl.BlockSpec(memory_space=pltpu.VMEM)
    smem = pl.BlockSpec(memory_space=pltpu.SMEM)
    dma = pltpu.SemaphoreType.DMA
    V = pltpu.VMEM
    scratch = [
        V((members, ext, width), BF16),
        V((members, points, width), BF16),
        V((members, ext, 2 * width), BF16),
        V((2 * points, ext), F32),
        V((members * pairs, 2 * points, ext), F32),
        V((members, points, width), F32),
        V((members * points, width), BF16),
        V((members, points, width), BF16),
        V((members, points, width), BF16),
        V((members, ext, 2 * width), BF16),
        V((n_ens, members, points, LANES), F32),
        V((n_ens, n_grid) + chunk, BF16),
        V((n_far, n_grid) + chunk, BF16),
        V((max(1, n_far - 1), n_grid) + chunk, BF16),
        V((max(1, n_far - 1), n_grid) + chunk, BF16),
        V((n_grid,) + chunk, BF16),
        V((n_grid,) + chunk, BF16),
        V((2, members, RIM, width), BF16),
        V((2, members, RIM, width), BF16),
        V((n_ens, 8, LANES), F32),
        V((n_grid, 8, LANES), F32),
        dma((2,)), dma((2,)),
        dma((n_ens,)), dma((n_ens,)),
        dma((n_far,)), dma((n_far,)),
        dma((n_far,)), dma((n_far,)),
        dma((n_grid,)), dma((n_grid,)),
        dma((2,)), dma((2,)),
        dma((n_ens,)), dma((n_ens,)),
        dma((n_grid,)), dma((n_grid,)),
    ]
    total, sens, grad_value, grad_dec = pl.pallas_call(
        functools.partial(kernel, n_ens, n_grid, channels),
        out_shape=(
            jax.ShapeDtypeStruct((8, LANES), F32),
            jax.ShapeDtypeStruct((members, points, width), F32),
            jax.ShapeDtypeStruct((rows_pp, width), F32),
            jax.ShapeDtypeStruct((rows_pp, LANES), F32),
        ),
        in_specs=[smem, smem] + [vmem] * 5,
        out_specs=(vmem,) * 4,
        scratch_shapes=scratch,
        compiler_params=pltpu.CompilerParams(
            collective_id=0, has_side_effects=True, vmem_limit_bytes=60 * 1024 * 1024
        ),
    )(adjacent_blocks, companion_matrix, embeddings, target, attention_matrix, readout, weight)
    count = n_ens * members * channels * (points // SCORED_ENTRIES) * n_grid
    return (
        total[0, 0] / count,
        sens,
        grad_value.reshape(-1),
        grad_dec[:, :channels].reshape(-1),
    )


def solution(mesh):
    in_specs = (
        P("ens", "grid", None),
        P(None, "grid"),
        P(),
        P(),
        P("grid", None),
        P(),
        P("grid"),
        P("grid"),
    )
    out_specs = (P(), P("ens", "grid", None), P(("ens", "grid")), P(("ens", "grid")))
    return jax.shard_map(
        per_device, mesh=mesh, in_specs=in_specs, out_specs=out_specs, check_vma=False
    )
```

time: 447 us -> 118 us (0.26); the launches traced: 441 us -> 117 us
  waiting for transfers between devices: 132 us -> 0 us
  matrix products: 122 us -> 0 us
  Pallas kernels: 0 us -> 103 us
  local copies, waits for them, and re-layouts: 83.5 us -> 10.6 us
  blocking collectives: 46.3 us -> 0 us
  other arithmetic: 26.1 us -> 0.72 us
  between operations: 17.7 us -> 2.44 us
  starting transfers between devices: 13 us -> 0 us
    dot_general x16 -> x0, matrix products: 122 us -> none  [the longest x1 30.9 us: per_device(): jnp.einsum('mbhqk,mbqhe->mbkhe', grad_scores, query_blocks, preferred_ele...]
    pallas_call x0 -> x1, Pallas kernels: none -> 103 us  [per_device(): pl.pallas_call(functools.partial(kernel, n_ens, n_grid, channels), out_sh...]
    unnamed x3 -> x0, waiting for transfers between devices: 61 us -> none
    ppermute x4 -> x0, waiting for transfers between devices: 50 us -> none  [the longest x2 39.8 us: passed_along(): lax.ppermute(value, axis, [(source, source + steps) for source in range(l...]
    psum x1 -> x0, blocking collectives: 39.7 us -> none  [per_device(): total = lax.psum(local_total, ('ens', 'grid'))]
    reshape x10 -> x1, local copies, waits for them, and re-layouts: 26 us -> 1.42 us  [per_device(): grad_dec[:, :channels].reshape(-1)]
    gather x4 -> x0, local copies, waits for them, and re-layouts: 21.4 us -> none  [per_device(): jnp.take(ext_view, local_slots, axis=1)]
    reduce_scatter x1 -> x0, waiting for transfers between devices: 21.2 us -> none  [per_device(): lax.psum_scatter(outgoing, 'ens', scatter_dimension=0, tiled=True)]
  transfers between devices with their start and end apart: 6 -> 0, of which waited for: 5 -> 0; matrix products, arithmetic and copies ran while one was open for 13% -> 0% of each run, Pallas kernels for 0% -> 0%
where the time goes in v1:
time: 118 us; the launch traced here: 117 us
  Pallas kernels  103 us (87%)
  local copies, waits for them, and re-layouts  10.6 us (9%)
  between operations  2.44 us (2%)
    pallas_call x1, Pallas kernels, per_device(): pl.pallas_call(functools.partial(kernel, n_ens, n_grid, channels), out_sh...  103 us
    unnamed x4, local copies, waits for them, and re-layouts  5.9 us

profile of v1, /device:TPU:16, one launch (start us, length us, event | category | flops | bytes accessed | tf_op | source)
XLA Modules:
  0.0 116.6 jit_solution(5431858295490232801)
XLA Ops:
  0.6 0.7 multiply_bitcast_fusion
  1.3 0.7 copy.14.weight_ref
  2.1 0.9 copy.12
  3.0 0.6 pad.8.ref_ref
  3.6 1.1 copy.13
  4.8 0.8 pad.9.r_ref
  5.5 102.8 %shard_map.111 = (f32[8,128]{1,0:T(8,128)}, f32[2,128,1024]{2,1,0:T(8,128)}, f32[32,1024]{1,0:T(8,128)}, f32[32,128]{1,0:T(8,128)}) custom-call(s32[2,3]{1,0:T(2,128)} %adj_ref.1, s32[7,8]{1,0:T(8,128)} %comp_ref.1, bf16[2,128,1024]{2,1,0:T(8,128)(2,1)} %x_ref.1, f32[128,128]{1,0:T(8,128)} %pad.8.ref_ref, bf16[1024,3072]{1,0:T(8,128)(2,1)} %w_ref.1, ...), custom_call_target="tpu_custom_call" | custom-call | tf_op jit(solution)/shard_map/pallas_call | solution.py:462
  108.4 1.2 %slice.6 = f32[1,1]{1,0:T(1,128)} slice(f32[8,128]{1,0:T(8,128)} %get-tuple-element.8), slice={[0:1], [0:1]} | slice | bytes 8 | tf_op jit(solution)/shard_map/slice | solution.py:479
  110.2 1.4 %reshape.17 = f32[3200]{0:T(1024)} reshape(f32[32,100]{1,0:T(8,128)} %bitcast.10) | data formatting | bytes 25600 | tf_op jit(solution)/shard_map/reshape | solution.py:482
  111.6 1.6 %copy.15 = f32[4,8,8,128]{3,1,2,0:T(8,128)} copy(f32[4,8,8,128]{3,2,1,0:T(8,128)} %bitcast.9) | data formatting | bytes 262144
  113.2 2.3 %copy.17 = f32[2,128,1024]{2,1,0:T(8,128)} copy(f32[2,128,1024]{2,1,0:T(8,128)} %get-tuple-element.17) | data formatting | bytes 2097152

commit v2 on v1

v2 whole, which is shorter than its diff:
```python
import functools
import math

import jax
import jax.numpy as jnp
from jax import lax
from jax.experimental import pallas as pl
from jax.experimental.pallas import tpu as pltpu
from jax.sharding import PartitionSpec as P

HEADS = 16
QB = 64
R_BLK = 2
NB = 3
SCORED_ENTRIES = 128
NLAT = 721
EPSILON = 1e-06
RIM = R_BLK * QB
LANES = 128
NEG = -1e30

F32 = jnp.float32
BF16 = jnp.bfloat16
MESH = pl.DeviceIdType.MESH


def mm(a, b):
    return lax.dot_general(a, b, (((1,), (0,)), ((), ())), preferred_element_type=F32)


def mm_nt(a, b):
    return lax.dot_general(a, b, (((1,), (1,)), ((), ())), preferred_element_type=F32)


def mm_tn(a, b):
    return lax.dot_general(a, b, (((0,), (0,)), ((), ())), preferred_element_type=F32)


def rms_scale(values):
    return lax.rsqrt(jnp.mean(values * values, axis=-1, keepdims=True) + EPSILON)


def kernel(
    n_ens, n_grid, channels,
    adj_ref, comp_ref, x_ref, ref_ref, w_hbm, r_ref, land_ref, strip_ref,
    tot_ref, out_ref, gv_ref, gd_ref,
    w_ref, rt, tgt, wgts, nrm, nrm_t, q_s, kv, cnt_s, ac_s, ac_t, state, hid, hid_t, go, gq, gkv, fc,
    vp, rc0, s1, rc1, s2, r2, gnr, gnx, tq, tg,
    w_sem, halo_send, halo_recv, fc_send, fc_recv, core_send, core_recv,
    x_send, x_recv, g_send, g_recv, back_send, back_recv,
    tq_send, tq_recv, tg_send, tg_recv,
):
    members, points, width = x_ref.shape
    ext = points + 2 * RIM
    nblk = points // QB
    pairs = width // LANES
    rounds = comp_ref.shape[0]
    patches = points // SCORED_ENTRIES
    rows_pp = width // (n_ens * n_grid)
    fold = max(1, 16 // rows_pp)
    wide = width // fold
    n_far = n_ens // 2
    pieces = 2 if n_grid % 2 == 0 else 1
    per_piece = n_grid // pieces
    e = lax.axis_index("ens")
    g = lax.axis_index("grid")
    core = e % 2
    far = e // 2
    scale = 1.0 / math.sqrt(width // HEADS)

    def ens_copy(src, dst, ss, rs, to):
        return pltpu.make_async_remote_copy(
            src_ref=src, dst_ref=dst, send_sem=ss, recv_sem=rs,
            device_id={"ens": to}, device_id_type=MESH,
        )

    def grid_copy(src, dst, ss, rs, to):
        return pltpu.make_async_remote_copy(
            src_ref=src, dst_ref=dst, send_sem=ss, recv_sem=rs,
            device_id={"grid": to}, device_id_type=MESH,
        )

    w_copy = pltpu.make_async_copy(w_hbm, w_ref, w_sem)
    w_copy.start()
    barrier = pltpu.get_barrier_semaphore()
    for k in range(1, n_ens):
        pl.semaphore_signal(barrier, inc=1, device_id={"ens": (e + k) % n_ens}, device_id_type=MESH)
    for k in range(1, n_grid):
        pl.semaphore_signal(barrier, inc=1, device_id={"grid": (g + k) % n_grid}, device_id_type=MESH)

    @pl.when(g == 0)
    def _():
        nrm[:, :RIM] = jnp.zeros((members, RIM, width), BF16)

    @pl.when(g == n_grid - 1)
    def _():
        nrm[:, RIM + points :] = jnp.zeros((members, RIM, width), BF16)

    ups, downs = [], []
    for m in range(members):
        lat = x_ref[m].astype(F32)
        nrm[m, RIM : RIM + points] = (lat * rms_scale(lat)).astype(BF16)
        if m == 0:
            pl.semaphore_wait(barrier, n_ens + n_grid - 2)
        up = grid_copy(nrm.at[m, pl.ds(points, RIM)], nrm.at[m, pl.ds(0, RIM)],
                       halo_send.at[m], halo_recv.at[m], (g + 1) % n_grid)
        down = grid_copy(nrm.at[m, pl.ds(RIM, RIM)], nrm.at[m, pl.ds(RIM + points, RIM)],
                         halo_send.at[members + m], halo_recv.at[members + m],
                         (g + n_grid - 1) % n_grid)
        pl.when(g < n_grid - 1)(up.start)
        pl.when(g > 0)(down.start)
        ups.append(up)
        downs.append(down)

    out_ref[...] = jnp.zeros(out_ref.shape, F32)
    out_ref[0, :channels] = r_ref[...].astype(F32)
    out_ref[1, :channels, :points] = ref_ref[...]
    rt[...] = out_ref[0, :LANES].astype(BF16)
    for j in range(patches):
        rows = slice(j * SCORED_ENTRIES, (j + 1) * SCORED_ENTRIES)
        tgt[rows] = out_ref[1, :LANES, rows].T
        phase = (strip_ref[j : j + 1].astype(F32) + 0.5) * (math.pi / NLAT) - 0.5 * math.pi
        wrow = jnp.cos(phase) * (1.0 + land_ref[j : j + 1].astype(F32))
        wgts[rows] = jnp.broadcast_to(wrow, (LANES, SCORED_ENTRIES)).T

    col = lax.broadcasted_iota(jnp.int32, (1, ext), 1)
    for b in range(nblk):
        count = jnp.zeros((1, ext), F32)
        for n in range(NB):
            first = (adj_ref[b, n] - g * nblk + R_BLK) * QB
            count += jnp.where((col >= first) & (col < first + QB), 1.0, 0.0)
        rows = jnp.broadcast_to(count, (QB, ext))
        cnt_s[b * QB : (b + 1) * QB] = rows
        cnt_s[points + b * QB : points + (b + 1) * QB] = rows

    w_copy.wait()
    tile = 512

    @pl.loop(0, width // tile)
    def _(t):
        own = nrm[:, RIM : RIM + points].reshape(members * points, width)
        c = pl.multiple_of(t * tile, tile)
        q_s[:, :, pl.ds(c, tile)] = mm(own, w_ref[:, pl.ds(c, tile)]).astype(BF16).reshape(
            members, points, tile
        )

    @pl.loop(0, 2 * width // tile)
    def _(t):
        own = nrm[:, RIM : RIM + points].reshape(members * points, width)
        c = pl.multiple_of(t * tile, tile)
        wt = w_ref[:, pl.ds(pl.multiple_of(c + width, tile), tile)]
        kv[:, RIM : RIM + points, pl.ds(c, tile)] = mm(own, wt).astype(BF16).reshape(
            members, points, tile
        )

    head_a = lax.broadcasted_iota(jnp.int32, (points, LANES), 1) < LANES // 2

    def stacked(v):
        zero = jnp.zeros_like(v)
        return jnp.concatenate([jnp.where(head_a, v, zero), jnp.where(head_a, zero, v)], axis=0)

    def merged(v):
        return jnp.where(head_a, v[:points], v[points:])

    group = 2

    def cols(c):
        c = pl.multiple_of(c * LANES, LANES)
        return pl.ds(c, LANES), pl.ds(pl.multiple_of(c + width, LANES), LANES)

    sends = []
    for m in range(members):
        pl.when(g > 0)(ups[m].wait_recv)
        pl.when(g < n_grid - 1)(downs[m].wait_recv)

        @pl.loop(0, 2 * width // tile)
        def _(t):
            c = pl.multiple_of(t * tile, tile)
            wt = w_ref[:, pl.ds(pl.multiple_of(c + width, tile), tile)]
            rim = jnp.concatenate([nrm[m, :RIM], nrm[m, RIM + points :]], axis=0)
            res = mm(rim, wt).astype(BF16)
            kv[m, :RIM, pl.ds(c, tile)] = res[:RIM]
            kv[m, RIM + points :, pl.ds(c, tile)] = res[RIM:]

        @pl.loop(0, pairs // group)
        def _(it):
            cnt = cnt_s[...]
            at = [cols(it * group + i) for i in range(group)]
            ss = [mm_nt(stacked(q_s[m, :, ck]), kv[m, :, ck]) for ck, _ in at]
            ss = [jnp.where(cnt > 0.0, s * scale, NEG) for s in ss]
            ex = [jnp.exp(s - jnp.max(s, axis=-1, keepdims=True)) * cnt for s in ss]
            aa = [x * (1.0 / jnp.sum(x, axis=-1, keepdims=True)) for x in ex]
            res = [merged(mm(a.astype(BF16), kv[m, :, cv])) for a, (_, cv) in zip(aa, at)]
            for i in range(group):
                ac_s[m * pairs + it * group + i] = aa[i]
                state[m, :, at[i][0]] = res[i]

        st = x_ref[m].astype(F32) + state[m]
        state[m] = st
        h = (st * rms_scale(st)).astype(BF16)
        hid[m * points : (m + 1) * points] = h
        fc[e, m] = mm_nt(h, rt[...])
        for k in range(1, n_ens):
            i = m * n_ens + k
            cp = ens_copy(fc.at[e, m], fc.at[e, m], fc_send.at[i], fc_recv.at[i], (e + k) % n_ens)
            cp.start()
            sends.append(cp)

    @pl.loop(0, members * pairs)
    def _(it):
        ac_t[it] = ac_s[it].astype(BF16).T

    for m in range(members):
        nrm_t[m] = nrm[m].T
    hid_t[...] = hid[...].T

    for cp in sends:
        cp.wait()

    lane = lax.broadcasted_iota(jnp.int32, (1, LANES), 1)
    valid = lane < channels
    total = jnp.zeros((1, LANES), F32)
    g16 = []
    for m in range(members):
        parts = []
        for j in range(patches):
            rows = slice(j * SCORED_ENTRIES, (j + 1) * SCORED_ENTRIES)
            rnd = (lane + g * patches + j) % rounds
            partner = jnp.zeros((1, LANES), jnp.int32)
            for r in range(rounds):
                partner = jnp.where(rnd == r, comp_ref[r, e * members + m], partner)
            f = fc[e, m, rows]
            pf = jnp.zeros_like(f)
            for n in range(n_ens * members):
                pf = jnp.where(partner == n, fc[n // members, n % members, rows], pf)
            wgt = wgts[rows]
            err = f - tgt[rows]
            dif = f - pf
            dt = jnp.sqrt(jnp.sum(wgt * err * err, axis=0, keepdims=True) + EPSILON)
            dp = jnp.sqrt(jnp.sum(wgt * dif * dif, axis=0, keepdims=True) + EPSILON)
            total += jnp.where(valid, dt - 0.5 * dp, 0.0)
            parts.append((wgt * err / dt - wgt * dif / dp).astype(BF16))
        g16.append(jnp.concatenate(parts, axis=0) if patches > 1 else parts[0])
    g_all = jnp.concatenate(g16, axis=0)

    tq[e] = jnp.broadcast_to(jnp.sum(total, axis=-1, keepdims=True), (8, LANES))
    tqs = []
    for k in range(1, n_ens):
        cp = ens_copy(tq.at[e], tq.at[e], tq_send.at[k], tq_recv.at[k], (e + k) % n_ens)
        cp.start()
        tqs.append(cp)

    for m in range(members):
        gh = mm(g16[m], rt[...])
        st = state[m]
        inv = rms_scale(st)
        y = st * inv
        gs = inv * (gh - y * jnp.mean(gh * y, axis=-1, keepdims=True))
        out_ref[m] = gs
        go[m] = gs.astype(BF16)

    for m in range(members):
        @pl.loop(0, pairs // group)
        def _(it):
            at = [cols(it * group + i) for i in range(group)]
            res = [mm(ac_t[m * pairs + it * group + i], stacked(go[m, :, at[i][0]])).astype(BF16)
                   for i in range(group)]
            for i in range(group):
                gkv[m, :, at[i][1]] = res[i]

    per_ens = width // n_ens

    def folded(v, count):
        v = v.reshape(n_grid, rows_pp, count)
        if fold > 1:
            step = count // fold
            v = jnp.concatenate([v[:, :, i * step : (i + 1) * step] for i in range(fold)], axis=1)
        return v.astype(BF16)

    @pl.loop(0, n_ens)
    def _(qd):
        d = pl.ds(pl.multiple_of(qd * per_ens, per_ens), per_ens)
        acc = mm(nrm_t[0, d], gkv[0, :, width:])
        for m in range(1, members):
            acc += mm(nrm_t[m, d], gkv[m, :, width:])
        vp[qd, :, :, :wide] = folded(acc, width)
        dec = mm(hid_t[d], g_all)
        if fold > 1:
            dec = jnp.concatenate(
                [dec, jnp.zeros((per_ens, LANES * (fold - 1)), F32)], axis=1
            )
        vp[qd, :, :, wide:] = folded(dec, LANES * fold)

    cores = []
    for k in range(n_far):
        f = (far + 1 + k) % n_far
        cp = ens_copy(vp.at[2 * f + 1 - core], rc0.at[f], core_send.at[k], core_recv.at[k],
                      2 * far + 1 - core)
        cp.start()
        cores.append(cp)

    for cp in tqs:
        cp.wait()
    tg[g] = functools.reduce(lambda a, b: a + b, [tq[i] for i in range(n_ens)])
    tgs = []
    for k in range(1, n_grid):
        cp = grid_copy(tg.at[g], tg.at[g], tg_send.at[k], tg_recv.at[k], (g + k) % n_grid)
        cp.start()
        tgs.append(cp)

    def back(m, start, stop):
        @pl.loop(start, stop)
        def _(it):
            at = [cols(it * group + i) for i in range(group)]
            aa = [ac_s[m * pairs + it * group + i] for i in range(group)]
            da = [mm_nt(stacked(go[m, :, ck]), kv[m, :, cv]) for ck, cv in at]
            ds = [a * (d - jnp.sum(a * d, axis=-1, keepdims=True)) * scale for a, d in zip(aa, da)]
            ds = [d.astype(BF16) for d in ds]
            dq = [merged(mm(d, kv[m, :, ck])).astype(BF16) for d, (ck, _) in zip(ds, at)]
            dk = [mm_tn(d, stacked(q_s[m, :, ck])).astype(BF16) for d, (ck, _) in zip(ds, at)]
            for i in range(group):
                gq[m, :, at[i][0]] = dq[i]
                gkv[m, :, at[i][0]] = dk[i]

    dt_tile = 256

    to_prev, to_next = [], []

    def rim_back(m):
        @pl.loop(0, width // dt_tile)
        def _(t):
            d = pl.ds(pl.multiple_of(t * dt_tile, dt_tile), dt_tile)
            rim = jnp.concatenate([gkv[m, :RIM], gkv[m, RIM + points :]], axis=0)
            res = mm_nt(rim, w_ref[d, width:]).astype(BF16)
            gnr[m, :, :, d] = res.reshape(2, RIM, dt_tile)

        prev = grid_copy(gnr.at[m, 0], gnx.at[m, 0], back_send.at[m], back_recv.at[m],
                         (g + n_grid - 1) % n_grid)
        nxt = grid_copy(gnr.at[m, 1], gnx.at[m, 1], back_send.at[members + m],
                        back_recv.at[members + m], (g + 1) % n_grid)
        pl.when(g > 0)(prev.start)
        pl.when(g < n_grid - 1)(nxt.start)
        to_prev.append(prev)
        to_next.append(nxt)

    xs = []

    def far_stage():
        for k in range(n_far - 1):
            cores[k].wait()
            f = (far + 1 + k) % n_far
            for c in range(pieces):
                sl = pl.ds(c * per_piece, per_piece)
                s1[k, sl] = (vp[2 * f + core, sl].astype(F32) + rc0[f, sl].astype(F32)).astype(BF16)
                cp = ens_copy(s1.at[k, sl], rc1.at[k, sl], x_send.at[k * pieces + c],
                              x_recv.at[k * pieces + c], 2 * f + core)
                cp.start()
                xs.append(cp)
        cores[n_far - 1].wait()

    gcs = [
        grid_copy(s2.at[(g + k) % n_grid], r2.at[k], g_send.at[k], g_recv.at[k], (g + k) % n_grid)
        for k in range(1, n_grid)
    ]

    def grid_stage(c):
        lo = c * per_piece
        sl = pl.ds(lo, per_piece)
        part = vp[2 * far + core, sl].astype(F32) + rc0[far, sl].astype(F32)
        for k in range(n_far - 1):
            xs[k * pieces + c].wait()
            part += rc1[k, sl].astype(F32)
        s2[sl] = part.astype(BF16)
        for k in range(1, n_grid):
            to = (g + k) % n_grid
            pl.when((to >= lo) & (to < lo + per_piece))(gcs[k - 1].start)

    steps = pairs // group
    for m in range(members):
        if m == 0:
            back(m, 0, 1)
            far_stage()
            back(m, 1, steps)
        elif m == 1:
            grid_stage(0)
            back(m, 0, steps // 2)
            for c in range(1, pieces):
                grid_stage(c)
            back(m, steps // 2, steps)
        else:
            back(m, 0, steps)
        rim_back(m)
    if members == 1:
        for c in range(pieces):
            grid_stage(c)

    @pl.loop(0, width // dt_tile)
    def _(t):
        d = pl.ds(pl.multiple_of(t * dt_tile, dt_tile), dt_tile)
        res = mm_nt(gq[...].reshape(members * points, width), w_ref[d, :width])
        res += mm_nt(gkv[:, RIM : RIM + points].reshape(members * points, 2 * width),
                     w_ref[d, width:])
        state[:, :, d] = res.reshape(members, points, dt_tile)

    for cp in tgs:
        cp.wait()
    whole = functools.reduce(lambda a, b: a + b, [tg[i] for i in range(n_grid)])
    count = n_ens * members * channels * patches * n_grid
    tot_ref[...] = whole * (1.0 / count)

    for m in range(members):
        @pl.when(g < n_grid - 1)
        def _():
            to_prev[m].wait_recv()
            state[m, points - RIM :] += gnx[m, 0].astype(F32)

        @pl.when(g > 0)
        def _():
            to_next[m].wait_recv()
            state[m, :RIM] += gnx[m, 1].astype(F32)

        lat = x_ref[m].astype(F32)
        inv = rms_scale(lat)
        y = lat * inv
        gn = state[m]
        out_ref[m] += inv * (gn - y * jnp.mean(gn * y, axis=-1, keepdims=True))

    for cp in gcs:
        cp.wait()
    acc = s2[g].astype(F32)
    for k in range(1, n_grid):
        acc += r2[k].astype(F32)
    for i in range(fold):
        for c in range(wide // LANES):
            gv_ref[:, i * (wide // LANES) + c] = acc[
                i * rows_pp : (i + 1) * rows_pp, c * LANES : (c + 1) * LANES
            ]
    gd_ref[...] = acc[:rows_pp, wide:]

    for m in range(members):
        @pl.when(g < n_grid - 1)
        def _():
            ups[m].wait_send()
            to_next[m].wait_send()

        @pl.when(g > 0)
        def _():
            downs[m].wait_send()
            to_prev[m].wait_send()


def per_device(
    embeddings,
    reference_analysis,
    attention_matrix,
    readout_matrix,
    adjacent_blocks,
    companion_matrix,
    continent_indicator,
    zonal_strip,
):
    members, points, width = embeddings.shape
    channels = reference_analysis.shape[0]
    n_ens, n_grid = lax.axis_size("ens"), lax.axis_size("grid")
    ext = points + 2 * RIM
    pairs = width // LANES
    rows_pp = width // (n_ens * n_grid)
    fold = max(1, 16 // rows_pp)
    chunk = (rows_pp * fold, width // fold + LANES)
    n_far = n_ens // 2
    patches = points // SCORED_ENTRIES
    pieces = 2 if n_grid % 2 == 0 else 1
    vmem = pl.BlockSpec(memory_space=pltpu.VMEM)
    smem = pl.BlockSpec(memory_space=pltpu.SMEM)
    dma = pltpu.SemaphoreType.DMA
    V = pltpu.VMEM
    scratch = [
        V((width, 3 * width), BF16),
        V((LANES, width), BF16),
        V((points, LANES), F32),
        V((points, LANES), F32),
        V((members, ext, width), BF16),
        V((members, width, ext), BF16),
        V((members, points, width), BF16),
        V((members, ext, 2 * width), BF16),
        V((2 * points, ext), F32),
        V((members * pairs, 2 * points, ext), F32),
        V((members * pairs, ext, 2 * points), BF16),
        V((members, points, width), F32),
        V((members * points, width), BF16),
        V((width, members * points), BF16),
        V((members, points, width), BF16),
        V((members, points, width), BF16),
        V((members, ext, 2 * width), BF16),
        V((n_ens, members, points, LANES), F32),
        V((n_ens, n_grid) + chunk, BF16),
        V((n_far, n_grid) + chunk, BF16),
        V((max(1, n_far - 1), n_grid) + chunk, BF16),
        V((max(1, n_far - 1), n_grid) + chunk, BF16),
        V((n_grid,) + chunk, BF16),
        V((n_grid,) + chunk, BF16),
        V((members, 2, RIM, width), BF16),
        V((members, 2, RIM, width), BF16),
        V((n_ens, 8, LANES), F32),
        V((n_grid, 8, LANES), F32),
        dma(()),
        dma((2 * members,)), dma((2 * members,)),
        dma((members * n_ens,)), dma((members * n_ens,)),
        dma((n_far,)), dma((n_far,)),
        dma((n_far * pieces,)), dma((n_far * pieces,)),
        dma((n_grid,)), dma((n_grid,)),
        dma((2 * members,)), dma((2 * members,)),
        dma((n_ens,)), dma((n_ens,)),
        dma((n_grid,)), dma((n_grid,)),
    ]
    total, sens, grad_value, grad_dec = pl.pallas_call(
        functools.partial(kernel, n_ens, n_grid, channels),
        out_shape=(
            jax.ShapeDtypeStruct((8, LANES), F32),
            jax.ShapeDtypeStruct((members, points, width), F32),
            jax.ShapeDtypeStruct((rows_pp, width // LANES, LANES), F32),
            jax.ShapeDtypeStruct((rows_pp, LANES), F32),
        ),
        in_specs=[smem, smem, vmem, vmem, pl.BlockSpec(memory_space=pl.ANY), vmem, vmem, vmem],
        out_specs=(vmem,) * 4,
        scratch_shapes=scratch,
        compiler_params=pltpu.CompilerParams(
            collective_id=0, has_side_effects=True, vmem_limit_bytes=60 * 1024 * 1024
        ),
    )(
        adjacent_blocks,
        companion_matrix,
        embeddings,
        reference_analysis,
        attention_matrix,
        readout_matrix.T,
        continent_indicator.reshape(patches, SCORED_ENTRIES),
        zonal_strip.reshape(patches, SCORED_ENTRIES),
    )
    return (
        total[0, 0],
        sens,
        grad_value.reshape(-1),
        grad_dec[:, :channels].reshape(-1),
    )


def solution(mesh):
    in_specs = (
        P("ens", "grid", None),
        P(None, "grid"),
        P(),
        P(),
        P("grid", None),
        P(),
        P("grid"),
        P("grid"),
    )
    out_specs = (P(), P("ens", "grid", None), P(("ens", "grid")), P(("ens", "grid")))
    return jax.shard_map(
        per_device, mesh=mesh, in_specs=in_specs, out_specs=out_specs, check_vma=False
    )
```

time: 118 us -> 89.9 us (0.76)
  Pallas kernels: 103 us -> 82.4 us
  local copies, waits for them, and re-layouts: 10.6 us -> 6.48 us
  between operations: 2.44 us -> 0.64 us
    pallas_call x1, Pallas kernels: 103 us -> 82.4 us  [per_device(): pl.pallas_call(functools.partial(kernel, n_ens, n_grid, channels), out_sh...]
    unnamed x4 -> x2, local copies, waits for them, and re-layouts: 5.9 us -> 3.87 us
    pad x2 -> x0, local copies, waits for them, and re-layouts: 1.4 us -> none  [the longest x1 0.76 us: per_device(): readout = jnp.pad(readout_matrix, ((0, 0), (0, LANES - channels)))]
where the time goes in v2:
time: 89.9 us; the launch traced here: 89.5 us
  Pallas kernels  82.4 us (92%)
  local copies, waits for them, and re-layouts  6.48 us (7%)
    pallas_call x1, Pallas kernels, per_device(): pl.pallas_call(functools.partial(kernel, n_ens, n_grid, channels), out_sh...  82.4 us
    unnamed x2, local copies, waits for them, and re-layouts  3.87 us

profile of v2, /device:TPU:16, one launch (start us, length us, event | category | flops | bytes accessed | tf_op | source)
XLA Modules:
  0.0 89.5 jit_solution(1649278113067303048)
XLA Ops:
  0.6 82.4 %shard_map.111 = (f32[8,128]{1,0:T(8,128)}, f32[2,128,1024]{2,1,0:T(8,128)}, f32[32,8,128]{2,1,0:T(8,128)}, f32[32,128]{1,0:T(8,128)}) custom-call(s32[2,3]{1,0:T(2,128)} %adj_ref.1, s32[7,8]{1,0:T(8,128)} %comp_ref.1, bf16[2,128,1024]{2,1,0:T(8,128)(2,1)} %x_ref.1, f32[100,128]{1,0:T(8,128)} %ref_ref.1, bf16[1024,3072]{1,0:T(8,128)(2,1)} %w_hbm.1, ...), custom_call_target="tpu_custom_call" | custom-call | tf_op jit(solution)/shard_map/pallas_call | solution.py:516
  83.0 1.2 %slice.6 = f32[1,1]{1,0:T(1,128)} slice(f32[8,128]{1,0:T(8,128)} %get-tuple-element.8), slice={[0:1], [0:1]} | slice | bytes 8 | tf_op jit(solution)/shard_map/slice | solution.py:541
  84.2 1.4 %reshape.23 = f32[3200]{0:T(1024)} reshape(f32[32,100]{1,0:T(8,128)} %bitcast.8) | data formatting | bytes 25600 | tf_op jit(solution)/shard_map/reshape | solution.py:544
  85.6 2.3 %copy.14 = f32[2,128,1024]{2,1,0:T(8,128)} copy(f32[2,128,1024]{2,1,0:T(8,128)} %get-tuple-element.17) | data formatting | bytes 2097152
  88.0 1.6 %copy.15 = f32[32768]{0:T(1024)} copy(f32[32768]{0:T(1024)} %bitcast.7) | data formatting | bytes 262144

commit v3 on v2

--- a/solution.py
+++ b/solution.py
@@ -45,7 +45,7 @@
     adj_ref, comp_ref, x_ref, ref_ref, w_hbm, r_ref, land_ref, strip_ref,
     tot_ref, out_ref, gv_ref, gd_ref,
     w_ref, rt, tgt, wgts, nrm, nrm_t, q_s, kv, cnt_s, ac_s, ac_t, state, hid, hid_t, go, gq, gkv, fc,
-    vp, rc0, s1, rc1, s2, r2, gnr, gnx, tq, tg,
+    vp, rc0, s1, rc1, s2, r2, gnr, gx, hand, gnx, ds_s, tq, tg,
     w_sem, halo_send, halo_recv, fc_send, fc_recv, core_send, core_recv,
     x_send, x_recv, g_send, g_recv, back_send, back_recv,
     tq_send, tq_recv, tg_send, tg_recv,
@@ -96,21 +96,33 @@
     def _():
         nrm[:, RIM + points :] = jnp.zeros((members, RIM, width), BF16)
 
-    ups, downs = [], []
+    odd = g % 2
+    far_row = RIM + points
+    near_src = pl.ds(pl.multiple_of((1 - odd) * far_row, RIM), RIM)
+    away = pl.ds(pl.multiple_of(odd * far_row, RIM), RIM)
+    mate = g + 1 - 2 * odd
+    onward = g + 2 - 4 * odd
+    back_to = g - 2 + 4 * odd
+    has_onward = (onward >= 0) & (onward < n_grid)
+    has_back = (back_to >= 0) & (back_to < n_grid)
+    onward_id = (onward + n_grid) % n_grid
+    back_id = (back_to + n_grid) % n_grid
+    swaps, passes = [], []
     for m in range(members):
         lat = x_ref[m].astype(F32)
         nrm[m, RIM : RIM + points] = (lat * rms_scale(lat)).astype(BF16)
         if m == 0:
             pl.semaphore_wait(barrier, n_ens + n_grid - 2)
-        up = grid_copy(nrm.at[m, pl.ds(points, RIM)], nrm.at[m, pl.ds(0, RIM)],
-                       halo_send.at[m], halo_recv.at[m], (g + 1) % n_grid)
-        down = grid_copy(nrm.at[m, pl.ds(RIM, RIM)], nrm.at[m, pl.ds(RIM + points, RIM)],
-                         halo_send.at[members + m], halo_recv.at[members + m],
-                         (g + n_grid - 1) % n_grid)
-        pl.when(g < n_grid - 1)(up.start)
-        pl.when(g > 0)(down.start)
-        ups.append(up)
-        downs.append(down)
+        cp = grid_copy(nrm.at[m, pl.ds(RIM, RIM)], nrm.at[m, away],
+                       halo_send.at[m], halo_recv.at[m], mate)
+        cp.start()
+        swaps.append(cp)
+        passes.append(grid_copy(nrm.at[m, near_src], nrm.at[m, away],
+                                halo_send.at[members + m], halo_recv.at[members + m], onward_id))
+
+    def pass_on(m):
+        swaps[m].wait_recv()
+        pl.when(has_onward)(passes[m].start)
 
     out_ref[...] = jnp.zeros(out_ref.shape, F32)
     out_ref[0, :channels] = r_ref[...].astype(F32)
@@ -144,6 +156,8 @@
             members, points, tile
         )
 
+    pass_on(0)
+
     @pl.loop(0, 2 * width // tile)
     def _(t):
         own = nrm[:, RIM : RIM + points].reshape(members * points, width)
@@ -153,6 +167,16 @@
             members, points, tile
         )
 
+    for m in range(1, members):
+        pass_on(m)
+
+    @pl.loop(0, 2 * width // tile)
+    def _(t):
+        near = nrm[:, near_src].reshape(members * RIM, width)
+        c = pl.multiple_of(t * tile, tile)
+        wt = w_ref[:, pl.ds(pl.multiple_of(c + width, tile), tile)]
+        kv[:, near_src, pl.ds(c, tile)] = mm(near, wt).astype(BF16).reshape(members, RIM, tile)
+
     head_a = lax.broadcasted_iota(jnp.int32, (points, LANES), 1) < LANES // 2
 
     def stacked(v):
@@ -170,17 +194,13 @@
 
     sends = []
     for m in range(members):
-        pl.when(g > 0)(ups[m].wait_recv)
-        pl.when(g < n_grid - 1)(downs[m].wait_recv)
+        pl.when(has_back)(passes[m].wait_recv)
 
         @pl.loop(0, 2 * width // tile)
         def _(t):
             c = pl.multiple_of(t * tile, tile)
             wt = w_ref[:, pl.ds(pl.multiple_of(c + width, tile), tile)]
-            rim = jnp.concatenate([nrm[m, :RIM], nrm[m, RIM + points :]], axis=0)
-            res = mm(rim, wt).astype(BF16)
-            kv[m, :RIM, pl.ds(c, tile)] = res[:RIM]
-            kv[m, RIM + points :, pl.ds(c, tile)] = res[RIM:]
+            kv[m, away, pl.ds(c, tile)] = mm(nrm[m, away], wt).astype(BF16)
 
         @pl.loop(0, pairs // group)
         def _(it):
@@ -316,15 +336,30 @@
             da = [mm_nt(stacked(go[m, :, ck]), kv[m, :, cv]) for ck, cv in at]
             ds = [a * (d - jnp.sum(a * d, axis=-1, keepdims=True)) * scale for a, d in zip(aa, da)]
             ds = [d.astype(BF16) for d in ds]
-            dq = [merged(mm(d, kv[m, :, ck])).astype(BF16) for d, (ck, _) in zip(ds, at)]
             dk = [mm_tn(d, stacked(q_s[m, :, ck])).astype(BF16) for d, (ck, _) in zip(ds, at)]
             for i in range(group):
+                ds_s[m * pairs + it * group + i] = ds[i]
+                gkv[m, :, at[i][0]] = dk[i]
+
+    def back_query(m):
+        @pl.loop(0, pairs // group)
+        def _(it):
+            at = [cols(it * group + i) for i in range(group)]
+            dq = [merged(mm(ds_s[m * pairs + it * group + i], kv[m, :, at[i][0]])).astype(BF16)
+                  for i in range(group)]
+            for i in range(group):
                 gq[m, :, at[i][0]] = dq[i]
-                gkv[m, :, at[i][0]] = dk[i]
 
     dt_tile = 256
 
-    to_prev, to_next = [], []
+    crosses = [
+        grid_copy(gnr.at[m, odd], gx.at[m], back_send.at[m], back_recv.at[m], back_id)
+        for m in range(members)
+    ]
+    hands = [
+        grid_copy(hand.at[m], gnx.at[m], back_send.at[members + m], back_recv.at[members + m], mate)
+        for m in range(members)
+    ]
 
     def rim_back(m):
         @pl.loop(0, width // dt_tile)
@@ -334,14 +369,17 @@
             res = mm_nt(rim, w_ref[d, width:]).astype(BF16)
             gnr[m, :, :, d] = res.reshape(2, RIM, dt_tile)
 
-        prev = grid_copy(gnr.at[m, 0], gnx.at[m, 0], back_send.at[m], back_recv.at[m],
-                         (g + n_grid - 1) % n_grid)
-        nxt = grid_copy(gnr.at[m, 1], gnx.at[m, 1], back_send.at[members + m],
-                        back_recv.at[members + m], (g + 1) % n_grid)
-        pl.when(g > 0)(prev.start)
-        pl.when(g < n_grid - 1)(nxt.start)
-        to_prev.append(prev)
-        to_next.append(nxt)
+        pl.when(has_back)(crosses[m].start)
+
+    def hand_over(m):
+        hand[m] = gnr[m, 1 - odd]
+
+        @pl.when(has_onward)
+        def _():
+            crosses[m].wait_recv()
+            hand[m] = (gnr[m, 1 - odd].astype(F32) + gx[m].astype(F32)).astype(BF16)
+
+        hands[m].start()
 
     xs = []
 
@@ -384,6 +422,7 @@
         elif m == 1:
             grid_stage(0)
             back(m, 0, steps // 2)
+            hand_over(0)
             for c in range(1, pieces):
                 grid_stage(c)
             back(m, steps // 2, steps)
@@ -394,6 +433,11 @@
         for c in range(pieces):
             grid_stage(c)
 
+    for m in range(members):
+        back_query(m)
+    for m in range(0 if members == 1 else 1, members):
+        hand_over(m)
+
     @pl.loop(0, width // dt_tile)
     def _(t):
         d = pl.ds(pl.multiple_of(t * dt_tile, dt_tile), dt_tile)
@@ -409,20 +453,11 @@
     tot_ref[...] = whole * (1.0 / count)
 
     for m in range(members):
-        @pl.when(g < n_grid - 1)
-        def _():
-            to_prev[m].wait_recv()
-            state[m, points - RIM :] += gnx[m, 0].astype(F32)
-
-        @pl.when(g > 0)
-        def _():
-            to_next[m].wait_recv()
-            state[m, :RIM] += gnx[m, 1].astype(F32)
-
+        hands[m].wait_recv()
         lat = x_ref[m].astype(F32)
         inv = rms_scale(lat)
         y = lat * inv
-        gn = state[m]
+        gn = state[m] + gnx[m].astype(F32)
         out_ref[m] += inv * (gn - y * jnp.mean(gn * y, axis=-1, keepdims=True))
 
     for cp in gcs:
@@ -438,15 +473,27 @@
     gd_ref[...] = acc[:rows_pp, wide:]
 
     for m in range(members):
-        @pl.when(g < n_grid - 1)
-        def _():
-            ups[m].wait_send()
-            to_next[m].wait_send()
-
-        @pl.when(g > 0)
-        def _():
-            downs[m].wait_send()
-            to_prev[m].wait_send()
+        swaps[m].wait_send()
+        hands[m].wait_send()
+        pl.when(has_onward)(passes[m].wait_send)
+        pl.when(has_back)(crosses[m].wait_send)
+
+
+def finish(channels, tot_in, sens_in, gv_in, gd_in, tot_ref, sens_ref, gv_ref, gd_ref):
+    tot_ref[...] = tot_in[:1, :1]
+    sens_ref[...] = sens_in[...]
+    gv_ref[...] = gv_in[...]
+    if gd_ref.shape[-1] != LANES:
+        gd_ref[...] = gd_in[:, :channels]
+        return
+    for i in range(gd_ref.shape[0]):
+        at, parts = i * LANES, []
+        while at < (i + 1) * LANES:
+            row, c = divmod(at, channels)
+            n = min(channels - c, (i + 1) * LANES - at)
+            parts.append(gd_in[row : row + 1, c : c + n])
+            at += n
+        gd_ref[i : i + 1] = jnp.concatenate(parts, axis=1)
 
 
 def per_device(
@@ -470,6 +517,7 @@
     n_far = n_ens // 2
     patches = points // SCORED_ENTRIES
     pieces = 2 if n_grid % 2 == 0 else 1
+    assert points == RIM and n_grid % 2 == 0
     vmem = pl.BlockSpec(memory_space=pltpu.VMEM)
     smem = pl.BlockSpec(memory_space=pltpu.SMEM)
     dma = pltpu.SemaphoreType.DMA
@@ -500,7 +548,10 @@
         V((n_grid,) + chunk, BF16),
         V((n_grid,) + chunk, BF16),
         V((members, 2, RIM, width), BF16),
-        V((members, 2, RIM, width), BF16),
+        V((members, RIM, width), BF16),
+        V((members, RIM, width), BF16),
+        V((members, RIM, width), BF16),
+        V((members * pairs, 2 * points, ext), BF16),
         V((n_ens, 8, LANES), F32),
         V((n_grid, 8, LANES), F32),
         dma(()),
@@ -537,11 +588,25 @@
         continent_indicator.reshape(patches, SCORED_ENTRIES),
         zonal_strip.reshape(patches, SCORED_ENTRIES),
     )
+    flat = rows_pp * channels
+    dec_shape = (flat // LANES, LANES) if flat % LANES == 0 else (rows_pp, channels)
+    total, sens, grad_value, grad_dec = pl.pallas_call(
+        functools.partial(finish, channels),
+        out_shape=(
+            jax.ShapeDtypeStruct((1, 1), F32),
+            jax.ShapeDtypeStruct(sens.shape, F32),
+            jax.ShapeDtypeStruct(grad_value.shape, F32),
+            jax.ShapeDtypeStruct(dec_shape, F32),
+        ),
+        in_specs=[vmem] * 4,
+        out_specs=(vmem,) * 4,
+        compiler_params=pltpu.CompilerParams(vmem_limit_bytes=60 * 1024 * 1024),
+    )(total, sens, grad_value, grad_dec)
     return (
-        total[0, 0],
+        total.reshape(()),
         sens,
         grad_value.reshape(-1),
-        grad_dec[:, :channels].reshape(-1),
+        grad_dec.reshape(-1),
     )
 
 

time: 89.9 us -> 86 us (0.957)
  local copies, waits for them, and re-layouts: 6.48 us -> 0 us
  Pallas kernels: 82.4 us -> 85.2 us
    unnamed x2 -> x0, local copies, waits for them, and re-layouts: 3.87 us -> none
    pallas_call x0 -> x1, Pallas kernels: none -> 2.33 us  [per_device(): pl.pallas_call(functools.partial(finish, channels), out_shape=(jax.ShapeD...]
    reshape x1 -> x0, local copies, waits for them, and re-layouts: 1.42 us -> none  [per_device(): grad_dec[:, :channels].reshape(-1)]
    slice x1 -> x0, local copies, waits for them, and re-layouts: 1.18 us -> none  [per_device(): total[0, 0]]
where the time goes in v3:
time: 86 us; the launch traced here: 85.9 us
  Pallas kernels  85.2 us (99%)
    pallas_call x1, Pallas kernels, per_device(): pl.pallas_call(functools.partial(kernel, n_ens, n_grid, channels), out_sh...  82.9 us
    pallas_call x1, Pallas kernels, per_device(): pl.pallas_call(functools.partial(finish, channels), out_shape=(jax.ShapeD...  2.33 us

profile of v3, /device:TPU:16, one launch (start us, length us, event | category | flops | bytes accessed | tf_op | source)
XLA Modules:
  0.0 85.9 jit_solution(15552096886430999371)
XLA Ops:
  0.6 82.9 %shard_map.111 = (f32[8,128]{1,0:T(8,128)}, f32[2,128,1024]{2,1,0:T(8,128)}, f32[32,8,128]{2,1,0:T(8,128)}, f32[32,128]{1,0:T(8,128)}) custom-call(s32[2,3]{1,0:T(2,128)} %adj_ref.1, s32[7,8]{1,0:T(8,128)} %comp_ref.1, bf16[2,128,1024]{2,1,0:T(8,128)(2,1)} %x_ref.1, f32[100,128]{1,0:T(8,128)} %ref_ref.1, bf16[1024,3072]{1,0:T(8,128)(2,1)} %w_hbm.1, ...), custom_call_target="tpu_custom_call" | custom-call | tf_op jit(solution)/shard_map/pallas_call | solution.py:567
  83.5 2.3 %shard_map.112 = (f32[1,1]{1,0:T(1,128)}, f32[2,128,1024]{2,1,0:T(8,128)}, f32[32,8,128]{2,1,0:T(8,128)}, f32[25,128]{1,0:T(8,128)}) custom-call(f32[8,128]{1,0:T(8,128)} %get-tuple-element.12.tot_in, f32[2,128,1024]{2,1,0:T(8,128)} %get-tuple-element.13.sens_in, f32[32,8,128]{2,1,0:T(8,128)} %get-tuple-element.14.gv_in, f32[32,128]{1,0:T(8,128)} %get-tuple-element.15.gd_in), custom_call_target="tpu_custom_call" | custom-call | tf_op jit(solution)/shard_map/pallas_call | solution.py:593

commit v4 on v3

--- a/solution.py
+++ b/solution.py
@@ -44,7 +44,7 @@
     n_ens, n_grid, channels,
     adj_ref, comp_ref, x_ref, ref_ref, w_hbm, r_ref, land_ref, strip_ref,
     tot_ref, out_ref, gv_ref, gd_ref,
-    w_ref, rt, tgt, wgts, nrm, nrm_t, q_s, kv, cnt_s, ac_s, ac_t, state, hid, hid_t, go, gq, gkv, fc,
+    w_ref, rt, tgt, wgts, nrm, nrm_t, q_s, kv, lc_s, ac_s, ac_t, state, hid, hid_t, go, gq, gkv, fc,
     vp, rc0, s1, rc1, s2, r2, gnr, gx, hand, gnx, ds_s, tq, tg,
     w_sem, halo_send, halo_recv, fc_send, fc_recv, core_send, core_recv,
     x_send, x_recv, g_send, g_recv, back_send, back_recv,
@@ -60,8 +60,7 @@
     fold = max(1, 16 // rows_pp)
     wide = width // fold
     n_far = n_ens // 2
-    pieces = 2 if n_grid % 2 == 0 else 1
-    per_piece = n_grid // pieces
+    half = n_grid // 2
     e = lax.axis_index("ens")
     g = lax.axis_index("grid")
     core = e % 2
@@ -141,9 +140,10 @@
         for n in range(NB):
             first = (adj_ref[b, n] - g * nblk + R_BLK) * QB
             count += jnp.where((col >= first) & (col < first + QB), 1.0, 0.0)
-        rows = jnp.broadcast_to(count, (QB, ext))
-        cnt_s[b * QB : (b + 1) * QB] = rows
-        cnt_s[points + b * QB : points + (b + 1) * QB] = rows
+        rows = jnp.where(count > 0.0, jnp.log(jnp.maximum(count, 1.0)), NEG)
+        rows = jnp.broadcast_to(rows, (QB, ext))
+        lc_s[b * QB : (b + 1) * QB] = rows
+        lc_s[points + b * QB : points + (b + 1) * QB] = rows
 
     w_copy.wait()
     tile = 512
@@ -152,9 +152,8 @@
     def _(t):
         own = nrm[:, RIM : RIM + points].reshape(members * points, width)
         c = pl.multiple_of(t * tile, tile)
-        q_s[:, :, pl.ds(c, tile)] = mm(own, w_ref[:, pl.ds(c, tile)]).astype(BF16).reshape(
-            members, points, tile
-        )
+        res = mm(own, w_ref[:, pl.ds(c, tile)]).astype(BF16) * scale
+        q_s[:, :, pl.ds(c, tile)] = res.astype(BF16).reshape(members, points, tile)
 
     pass_on(0)
 
@@ -204,11 +203,11 @@
 
         @pl.loop(0, pairs // group)
         def _(it):
-            cnt = cnt_s[...]
+            log_count = lc_s[...]
             at = [cols(it * group + i) for i in range(group)]
             ss = [mm_nt(stacked(q_s[m, :, ck]), kv[m, :, ck]) for ck, _ in at]
-            ss = [jnp.where(cnt > 0.0, s * scale, NEG) for s in ss]
-            ex = [jnp.exp(s - jnp.max(s, axis=-1, keepdims=True)) * cnt for s in ss]
+            ss = [s + log_count for s in ss]
+            ex = [jnp.exp(s - jnp.max(s, axis=-1, keepdims=True)) for s in ss]
             aa = [x * (1.0 / jnp.sum(x, axis=-1, keepdims=True)) for x in ex]
             res = [merged(mm(a.astype(BF16), kv[m, :, cv])) for a, (_, cv) in zip(aa, at)]
             for i in range(group):
@@ -292,6 +291,7 @@
 
     def folded(v, count):
         v = v.reshape(n_grid, rows_pp, count)
+        v = jnp.stack([v[i] for i in list(range(0, n_grid, 2)) + list(range(1, n_grid, 2))])
         if fold > 1:
             step = count // fold
             v = jnp.concatenate([v[:, :, i * step : (i + 1) * step] for i in range(fold)], axis=1)
@@ -334,7 +334,7 @@
             at = [cols(it * group + i) for i in range(group)]
             aa = [ac_s[m * pairs + it * group + i] for i in range(group)]
             da = [mm_nt(stacked(go[m, :, ck]), kv[m, :, cv]) for ck, cv in at]
-            ds = [a * (d - jnp.sum(a * d, axis=-1, keepdims=True)) * scale for a, d in zip(aa, da)]
+            ds = [a * (d - jnp.sum(a * d, axis=-1, keepdims=True)) for a, d in zip(aa, da)]
             ds = [d.astype(BF16) for d in ds]
             dk = [mm_tn(d, stacked(q_s[m, :, ck])).astype(BF16) for d, (ck, _) in zip(ds, at)]
             for i in range(group):
@@ -345,10 +345,10 @@
         @pl.loop(0, pairs // group)
         def _(it):
             at = [cols(it * group + i) for i in range(group)]
-            dq = [merged(mm(ds_s[m * pairs + it * group + i], kv[m, :, at[i][0]])).astype(BF16)
+            dq = [merged(mm(ds_s[m * pairs + it * group + i], kv[m, :, at[i][0]])) * scale
                   for i in range(group)]
             for i in range(group):
-                gq[m, :, at[i][0]] = dq[i]
+                gq[m, :, at[i][0]] = dq[i].astype(BF16)
 
     dt_tile = 256
 
@@ -383,59 +383,70 @@
 
     xs = []
 
+    def part_of(c):
+        return pl.ds(((1 - odd) if c == 0 else odd) * half, half)
+
     def far_stage():
         for k in range(n_far - 1):
             cores[k].wait()
             f = (far + 1 + k) % n_far
-            for c in range(pieces):
-                sl = pl.ds(c * per_piece, per_piece)
+            for c in range(2):
+                sl = part_of(c)
                 s1[k, sl] = (vp[2 * f + core, sl].astype(F32) + rc0[f, sl].astype(F32)).astype(BF16)
-                cp = ens_copy(s1.at[k, sl], rc1.at[k, sl], x_send.at[k * pieces + c],
-                              x_recv.at[k * pieces + c], 2 * f + core)
+                cp = ens_copy(s1.at[k, sl], rc1.at[k, sl], x_send.at[k * 2 + c],
+                              x_recv.at[k * 2 + c], 2 * f + core)
                 cp.start()
                 xs.append(cp)
         cores[n_far - 1].wait()
 
-    gcs = [
-        grid_copy(s2.at[(g + k) % n_grid], r2.at[k], g_send.at[k], g_recv.at[k], (g + k) % n_grid)
-        for k in range(1, n_grid)
-    ]
-
-    def grid_stage(c):
-        lo = c * per_piece
-        sl = pl.ds(lo, per_piece)
+    def part_sum(c):
+        sl = part_of(c)
         part = vp[2 * far + core, sl].astype(F32) + rc0[far, sl].astype(F32)
         for k in range(n_far - 1):
-            xs[k * pieces + c].wait()
+            xs[k * 2 + c].wait()
             part += rc1[k, sl].astype(F32)
-        s2[sl] = part.astype(BF16)
-        for k in range(1, n_grid):
-            to = (g + k) % n_grid
-            pl.when((to >= lo) & (to < lo + per_piece))(gcs[k - 1].start)
+        return part
+
+    mate_copy = grid_copy(s2.at[0], r2.at[0], g_send.at[0], g_recv.at[0], mate)
+    place = g // 2
+    gcs = [
+        grid_copy(s2.at[1, (place + k) % half], r2.at[1, k], g_send.at[k], g_recv.at[k],
+                  2 * ((place + k) % half) + odd)
+        for k in range(1, half)
+    ]
+
+    def mate_stage():
+        s2[0] = part_sum(0).astype(BF16)
+        mate_copy.start()
+
+    def grid_stage():
+        part = part_sum(1)
+        mate_copy.wait()
+        s2[1] = (part + r2[0].astype(F32)).astype(BF16)
+        for cp in gcs:
+            cp.start()
 
     steps = pairs // group
     for m in range(members):
         if m == 0:
             back(m, 0, 1)
             far_stage()
-            back(m, 1, steps)
+            back(m, 1, steps - 1)
+            mate_stage()
+            back(m, steps - 1, steps)
         elif m == 1:
-            grid_stage(0)
-            back(m, 0, steps // 2)
+            back(m, 0, 1)
+            grid_stage()
+            back(m, 1, 2)
             hand_over(0)
-            for c in range(1, pieces):
-                grid_stage(c)
-            back(m, steps // 2, steps)
+            back(m, 2, steps)
         else:
             back(m, 0, steps)
         rim_back(m)
-    if members == 1:
-        for c in range(pieces):
-            grid_stage(c)
 
     for m in range(members):
         back_query(m)
-    for m in range(0 if members == 1 else 1, members):
+    for m in range(1, members):
         hand_over(m)
 
     @pl.loop(0, width // dt_tile)
@@ -462,9 +473,9 @@
 
     for cp in gcs:
         cp.wait()
-    acc = s2[g].astype(F32)
-    for k in range(1, n_grid):
-        acc += r2[k].astype(F32)
+    acc = s2[1, place].astype(F32)
+    for k in range(1, half):
+        acc += r2[1, k].astype(F32)
     for i in range(fold):
         for c in range(wide // LANES):
             gv_ref[:, i * (wide // LANES) + c] = acc[
@@ -516,8 +527,7 @@
     chunk = (rows_pp * fold, width // fold + LANES)
     n_far = n_ens // 2
     patches = points // SCORED_ENTRIES
-    pieces = 2 if n_grid % 2 == 0 else 1
-    assert points == RIM and n_grid % 2 == 0
+    assert points == RIM and n_grid % 2 == 0 and members > 1
     vmem = pl.BlockSpec(memory_space=pltpu.VMEM)
     smem = pl.BlockSpec(memory_space=pltpu.SMEM)
     dma = pltpu.SemaphoreType.DMA
@@ -545,8 +555,8 @@
         V((n_far, n_grid) + chunk, BF16),
         V((max(1, n_far - 1), n_grid) + chunk, BF16),
         V((max(1, n_far - 1), n_grid) + chunk, BF16),
-        V((n_grid,) + chunk, BF16),
-        V((n_grid,) + chunk, BF16),
+        V((2, n_grid // 2) + chunk, BF16),
+        V((2, n_grid // 2) + chunk, BF16),
         V((members, 2, RIM, width), BF16),
         V((members, RIM, width), BF16),
         V((members, RIM, width), BF16),
@@ -558,7 +568,7 @@
         dma((2 * members,)), dma((2 * members,)),
         dma((members * n_ens,)), dma((members * n_ens,)),
         dma((n_far,)), dma((n_far,)),
-        dma((n_far * pieces,)), dma((n_far * pieces,)),
+        dma((n_far * 2,)), dma((n_far * 2,)),
         dma((n_grid,)), dma((n_grid,)),
         dma((2 * members,)), dma((2 * members,)),
         dma((n_ens,)), dma((n_ens,)),

time: 86 us -> 81.5 us (0.948); the launches traced: 85.9 us -> 79.9 us
  Pallas kernels: 85.2 us -> 79.3 us
    pallas_call x1, Pallas kernels: 82.9 us -> 76.9 us  [per_device(): pl.pallas_call(functools.partial(kernel, n_ens, n_grid, channels), out_sh...]
where the time goes in v4:
time: 81.5 us; the launch traced here: 79.9 us
  Pallas kernels  79.3 us (97%)
    pallas_call x1, Pallas kernels, per_device(): pl.pallas_call(functools.partial(kernel, n_ens, n_grid, channels), out_sh...  76.9 us
    pallas_call x1, Pallas kernels, per_device(): pl.pallas_call(functools.partial(finish, channels), out_shape=(jax.ShapeD...  2.33 us

profile of v4, /device:TPU:16, one launch (start us, length us, event | category | flops | bytes accessed | tf_op | source)
XLA Modules:
  0.0 79.9 jit_solution(10266945704980085238)
XLA Ops:
  0.6 76.9 %shard_map.111 = (f32[8,128]{1,0:T(8,128)}, f32[2,128,1024]{2,1,0:T(8,128)}, f32[32,8,128]{2,1,0:T(8,128)}, f32[32,128]{1,0:T(8,128)}) custom-call(s32[2,3]{1,0:T(2,128)} %adj_ref.1, s32[7,8]{1,0:T(8,128)} %comp_ref.1, bf16[2,128,1024]{2,1,0:T(8,128)(2,1)} %x_ref.1, f32[100,128]{1,0:T(8,128)} %ref_ref.1, bf16[1024,3072]{1,0:T(8,128)(2,1)} %w_hbm.1, ...), custom_call_target="tpu_custom_call" | custom-call | tf_op jit(solution)/shard_map/pallas_call | solution.py:577
  77.6 2.3 %shard_map.112 = (f32[1,1]{1,0:T(1,128)}, f32[2,128,1024]{2,1,0:T(8,128)}, f32[32,8,128]{2,1,0:T(8,128)}, f32[25,128]{1,0:T(8,128)}) custom-call(f32[8,128]{1,0:T(8,128)} %get-tuple-element.12.tot_in, f32[2,128,1024]{2,1,0:T(8,128)} %get-tuple-element.13.sens_in, f32[32,8,128]{2,1,0:T(8,128)} %get-tuple-element.14.gv_in, f32[32,128]{1,0:T(8,128)} %get-tuple-element.15.gd_in), custom_call_target="tpu_custom_call" | custom-call | tf_op jit(solution)/shard_map/pallas_call | solution.py:603

commit v5 on v4

--- a/solution.py
+++ b/solution.py
@@ -97,8 +97,14 @@
 
     odd = g % 2
     far_row = RIM + points
-    near_src = pl.ds(pl.multiple_of((1 - odd) * far_row, RIM), RIM)
-    away = pl.ds(pl.multiple_of(odd * far_row, RIM), RIM)
+    bit = RIM // 2
+
+    def near(h):
+        return pl.ds(pl.multiple_of((1 - odd) * far_row + h * bit, bit), bit)
+
+    def away(h):
+        return pl.ds(pl.multiple_of(odd * far_row + h * bit, bit), bit)
+
     mate = g + 1 - 2 * odd
     onward = g + 2 - 4 * odd
     back_to = g - 2 + 4 * odd
@@ -112,16 +118,19 @@
         nrm[m, RIM : RIM + points] = (lat * rms_scale(lat)).astype(BF16)
         if m == 0:
             pl.semaphore_wait(barrier, n_ens + n_grid - 2)
-        cp = grid_copy(nrm.at[m, pl.ds(RIM, RIM)], nrm.at[m, away],
-                       halo_send.at[m], halo_recv.at[m], mate)
-        cp.start()
-        swaps.append(cp)
-        passes.append(grid_copy(nrm.at[m, near_src], nrm.at[m, away],
-                                halo_send.at[members + m], halo_recv.at[members + m], onward_id))
-
-    def pass_on(m):
-        swaps[m].wait_recv()
-        pl.when(has_onward)(passes[m].start)
+        for h in range(2):
+            i = 2 * m + h
+            j = 2 * members + i
+            cp = grid_copy(nrm.at[m, pl.ds(RIM + h * bit, bit)], nrm.at[m, away(h)],
+                           halo_send.at[i], halo_recv.at[i], mate)
+            cp.start()
+            swaps.append(cp)
+            passes.append(grid_copy(nrm.at[m, near(h)], nrm.at[m, away(h)],
+                                    halo_send.at[j], halo_recv.at[j], onward_id))
+
+    def pass_on(m, h):
+        swaps[2 * m + h].wait_recv()
+        pl.when(has_onward)(passes[2 * m + h].start)
 
     out_ref[...] = jnp.zeros(out_ref.shape, F32)
     out_ref[0, :channels] = r_ref[...].astype(F32)
@@ -155,7 +164,8 @@
         res = mm(own, w_ref[:, pl.ds(c, tile)]).astype(BF16) * scale
         q_s[:, :, pl.ds(c, tile)] = res.astype(BF16).reshape(members, points, tile)
 
-    pass_on(0)
+    pass_on(0, 0)
+    pass_on(0, 1)
 
     @pl.loop(0, 2 * width // tile)
     def _(t):
@@ -166,16 +176,6 @@
             members, points, tile
         )
 
-    for m in range(1, members):
-        pass_on(m)
-
-    @pl.loop(0, 2 * width // tile)
-    def _(t):
-        near = nrm[:, near_src].reshape(members * RIM, width)
-        c = pl.multiple_of(t * tile, tile)
-        wt = w_ref[:, pl.ds(pl.multiple_of(c + width, tile), tile)]
-        kv[:, near_src, pl.ds(c, tile)] = mm(near, wt).astype(BF16).reshape(members, RIM, tile)
-
     head_a = lax.broadcasted_iota(jnp.int32, (points, LANES), 1) < LANES // 2
 
     def stacked(v):
@@ -193,13 +193,22 @@
 
     sends = []
     for m in range(members):
-        pl.when(has_back)(passes[m].wait_recv)
+        if m + 1 < members:
+            pass_on(m + 1, 0)
+        for h in range(2):
+            pl.when(has_back)(passes[2 * m + h].wait_recv)
 
         @pl.loop(0, 2 * width // tile)
         def _(t):
             c = pl.multiple_of(t * tile, tile)
             wt = w_ref[:, pl.ds(pl.multiple_of(c + width, tile), tile)]
-            kv[m, away, pl.ds(c, tile)] = mm(nrm[m, away], wt).astype(BF16)
+            rim = jnp.concatenate([nrm[m, :RIM], nrm[m, RIM + points :]], axis=0)
+            res = mm(rim, wt).astype(BF16)
+            kv[m, :RIM, pl.ds(c, tile)] = res[:RIM]
+            kv[m, RIM + points :, pl.ds(c, tile)] = res[RIM:]
+
+        if m + 1 < members:
+            pass_on(m + 1, 1)
 
         @pl.loop(0, pairs // group)
         def _(it):
@@ -352,14 +361,13 @@
 
     dt_tile = 256
 
-    crosses = [
-        grid_copy(gnr.at[m, odd], gx.at[m], back_send.at[m], back_recv.at[m], back_id)
-        for m in range(members)
-    ]
-    hands = [
-        grid_copy(hand.at[m], gnx.at[m], back_send.at[members + m], back_recv.at[members + m], mate)
-        for m in range(members)
-    ]
+    crosses, hands = [], []
+    for i in range(2 * members):
+        m, sl, j = i // 2, pl.ds((i % 2) * bit, bit), 2 * members + i
+        crosses.append(grid_copy(gnr.at[m, odd, sl], gx.at[m, sl],
+                                 back_send.at[i], back_recv.at[i], back_id))
+        hands.append(grid_copy(hand.at[m, sl], gnx.at[m, sl],
+                               back_send.at[j], back_recv.at[j], mate))
 
     def rim_back(m):
         @pl.loop(0, width // dt_tile)
@@ -369,17 +377,19 @@
             res = mm_nt(rim, w_ref[d, width:]).astype(BF16)
             gnr[m, :, :, d] = res.reshape(2, RIM, dt_tile)
 
-        pl.when(has_back)(crosses[m].start)
-
-    def hand_over(m):
-        hand[m] = gnr[m, 1 - odd]
+        for h in range(2):
+            pl.when(has_back)(crosses[2 * m + h].start)
+
+    def hand_over(m, h):
+        sl = pl.ds(h * bit, bit)
+        hand[m, sl] = gnr[m, 1 - odd, sl]
 
         @pl.when(has_onward)
         def _():
-            crosses[m].wait_recv()
-            hand[m] = (gnr[m, 1 - odd].astype(F32) + gx[m].astype(F32)).astype(BF16)
-
-        hands[m].start()
+            crosses[2 * m + h].wait_recv()
+            hand[m, sl] = (gnr[m, 1 - odd, sl].astype(F32) + gx[m, sl].astype(F32)).astype(BF16)
+
+        hands[2 * m + h].start()
 
     xs = []
 
@@ -438,7 +448,8 @@
             back(m, 0, 1)
             grid_stage()
             back(m, 1, 2)
-            hand_over(0)
+            hand_over(0, 0)
+            hand_over(0, 1)
             back(m, 2, steps)
         else:
             back(m, 0, steps)
@@ -446,8 +457,9 @@
 
     for m in range(members):
         back_query(m)
-    for m in range(1, members):
-        hand_over(m)
+        for late in range(1, members):
+            if m < 2:
+                hand_over(late, m)
 
     @pl.loop(0, width // dt_tile)
     def _(t):
@@ -464,7 +476,8 @@
     tot_ref[...] = whole * (1.0 / count)
 
     for m in range(members):
-        hands[m].wait_recv()
+        for h in range(2):
+            hands[2 * m + h].wait_recv()
         lat = x_ref[m].astype(F32)
         inv = rms_scale(lat)
         y = lat * inv
@@ -483,11 +496,11 @@
             ]
     gd_ref[...] = acc[:rows_pp, wide:]
 
-    for m in range(members):
-        swaps[m].wait_send()
-        hands[m].wait_send()
-        pl.when(has_onward)(passes[m].wait_send)
-        pl.when(has_back)(crosses[m].wait_send)
+    for i in range(2 * members):
+        swaps[i].wait_send()
+        hands[i].wait_send()
+        pl.when(has_onward)(passes[i].wait_send)
+        pl.when(has_back)(crosses[i].wait_send)
 
 
 def finish(channels, tot_in, sens_in, gv_in, gd_in, tot_ref, sens_ref, gv_ref, gd_ref):
@@ -565,12 +578,12 @@
         V((n_ens, 8, LANES), F32),
         V((n_grid, 8, LANES), F32),
         dma(()),
-        dma((2 * members,)), dma((2 * members,)),
+        dma((4 * members,)), dma((4 * members,)),
         dma((members * n_ens,)), dma((members * n_ens,)),
         dma((n_far,)), dma((n_far,)),
         dma((n_far * 2,)), dma((n_far * 2,)),
         dma((n_grid,)), dma((n_grid,)),
-        dma((2 * members,)), dma((2 * members,)),
+        dma((4 * members,)), dma((4 * members,)),
         dma((n_ens,)), dma((n_ens,)),
         dma((n_grid,)), dma((n_grid,)),
     ]

time: 81.5 us -> 81.8 us (level)
  the two profiles are of different devices: /device:TPU:16 before, /device:TPU:0 now
where the time goes in v5:
time: 81.8 us; the launch traced here: 81.7 us
  Pallas kernels  81 us (99%)
    pallas_call x1, Pallas kernels, per_device(): pl.pallas_call(functools.partial(kernel, n_ens, n_grid, channels), out_sh...  78.7 us
    pallas_call x1, Pallas kernels, per_device(): pl.pallas_call(functools.partial(finish, channels), out_shape=(jax.ShapeD...  2.33 us

profile of v5, /device:TPU:0, one launch (start us, length us, event | category | flops | bytes accessed | tf_op | source)
XLA Modules:
  0.0 81.7 jit_solution(17209630238042998566)
XLA Ops:
  0.6 78.7 %shard_map.111 = (f32[8,128]{1,0:T(8,128)}, f32[2,128,1024]{2,1,0:T(8,128)}, f32[32,8,128]{2,1,0:T(8,128)}, f32[32,128]{1,0:T(8,128)}) custom-call(s32[2,3]{1,0:T(2,128)} %adj_ref.1, s32[7,8]{1,0:T(8,128)} %comp_ref.1, bf16[2,128,1024]{2,1,0:T(8,128)(2,1)} %x_ref.1, f32[100,128]{1,0:T(8,128)} %ref_ref.1, bf16[1024,3072]{1,0:T(8,128)(2,1)} %w_hbm.1, ...), custom_call_target="tpu_custom_call" | custom-call | tf_op jit(solution)/shard_map/pallas_call | solution.py:590
  79.4 2.3 %shard_map.112 = (f32[1,1]{1,0:T(1,128)}, f32[2,128,1024]{2,1,0:T(8,128)}, f32[32,8,128]{2,1,0:T(8,128)}, f32[25,128]{1,0:T(8,128)}) custom-call(f32[8,128]{1,0:T(8,128)} %get-tuple-element.12.tot_in, f32[2,128,1024]{2,1,0:T(8,128)} %get-tuple-element.13.sens_in, f32[32,8,128]{2,1,0:T(8,128)} %get-tuple-element.14.gv_in, f32[32,128]{1,0:T(8,128)} %get-tuple-element.15.gd_in), custom_call_target="tpu_custom_call" | custom-call | tf_op jit(solution)/shard_map/pallas_call | solution.py:616
